TPU v7x, 32 devices: a whole 2x2x4 slice. The times are simulated.
32 devices in a mesh: dp: 16 (over z, y, x), head: 2 (over core).
Axes of the slice: x: 2, y: 2, z: 4, core: 2. Of those that a mesh axis runs over, the one named last changes fastest.
Arguments:
- tokens: bfloat16 [32768, 768], P(('dp', 'head')), may hold values from -6 to 6
- lengths: int32 [16, 32], P('dp'), may hold values from 1 to 512, 2048 in all within a row
- w_qkv: bfloat16 [768, 3, 768], P(None, None, 'head'), may hold values from -0.21875 to 0.21875
- bias_qv: float32 [768, 2], P('head'), may hold values from -4 to 4
- w_out: bfloat16 [768, 768], replicated, may hold values from -0.625 to 0.625
- bias_out: float32 [768], replicated, may hold values from -4 to 4
- ln1_gain: float32 [768], replicated, may hold values from 0.5 to 1.5
- ln1_bias: float32 [768], replicated, may hold values from -4 to 4
- w_in: bfloat16 [768, 3072], replicated, may hold values from -0.21875 to 0.21875
- bias_in: float32 [3072], replicated, may hold values from -4 to 4
- w_down: bfloat16 [3072, 768], replicated, may hold values from -0.109375 to 0.109375
- bias_down: float32 [768], replicated, may hold values from -4 to 4
- ln2_gain: float32 [768], replicated, may hold values from 0.5 to 1.5
- ln2_bias: float32 [768], replicated, may hold values from -4 to 4
- term_w: float32 [768], replicated, may hold values from -0.21875 to 0.21875
- term_bias: float32 [1], replicated, may hold values from -3 to 3
- grad_hidden: float32 [32768, 768], P(('dp', 'head')), may hold values from -6 to 6
- grad_term: float32 [32768], P(('dp', 'head')), may hold values from -6 to 6
Outputs:
- hidden_out: bfloat16 [32768, 768], P(('dp', 'head'))
- term_weight: float32 [32768], P(('dp', 'head'))
- grad_tokens: float32 [32768, 768], P(('dp', 'head'))
- grad_w_qkv: float32 [768, 3, 768], P('dp', None, 'head')
- grad_bias_qv: float32 [768, 2], P(('dp', 'head'))
- grad_w_out: float32 [768, 768], P(('dp', 'head'))
- grad_bias_out: float32 [768], P(('dp', 'head'))
- grad_ln1_gain: float32 [768], P(('dp', 'head'))
- grad_ln1_bias: float32 [768], P(('dp', 'head'))
- grad_w_in: float32 [768, 3072], P(('dp', 'head'))
- grad_bias_in: float32 [3072], P(('dp', 'head'))
- grad_w_down: float32 [3072, 768], P(('dp', 'head'))
- grad_bias_down: float32 [768], P(('dp', 'head'))
- grad_ln2_gain: float32 [768], P(('dp', 'head'))
- grad_ln2_bias: float32 [768], P(('dp', 'head'))
- grad_term_w: float32 [768], P(('dp', 'head'))
- grad_term_bias: float32 [1], replicated
Inputs may be any that keep to these rules, and one draw needn't show every extreme that they name: `lengths`: each row lists the 32 passages packed in order into one row of 2048 tokens; a row sums to 2048 and its largest length is exactly 512.
All inputs are finite; a program needn't handle non-finite values.
Results may differ from a plain program's by a relative error of at most 0.012.
The roundings to bfloat16 on the way count: a program that leaves them out, or rounds other values in their place, can miss the bound.
Values may be sent and summed in bfloat16 or wider, within the bound.
A program may use at most 256 MiB of HBM per device.

v0:
```python
from functools import partial

import jax
import jax.numpy as jnp
from jax import lax
from jax.sharding import PartitionSpec as P

MODEL_DIM = 768
HEAD_DIM = 64


highest = lax.Precision.HIGHEST
norm_eps = 1e-06


def segment_ids(lengths, row_len):
    boundary = jnp.cumsum(lengths, axis=-1)
    places = jnp.arange(row_len, dtype=jnp.int32)
    return jnp.sum((places[None, :, None] >= boundary[:, None, :]).astype(jnp.int32), axis=-1)


def layer_norm(resid, gain, shift):
    center = resid - jnp.mean(resid, axis=-1, keepdims=True)
    spread = jnp.mean(center * center, axis=-1, keepdims=True)
    return center * lax.rsqrt(spread + norm_eps) * gain + shift


def shards(
    tokens,
    lengths,
    w_qkv,
    bias_qv,
    w_out,
    bias_out,
    ln1_gain,
    ln1_bias,
    w_in,
    bias_in,
    w_down,
    bias_down,
    ln2_gain,
    ln2_bias,
    term_w,
    term_bias,
    grad_hidden,
    grad_term,
):
    group_rows = lax.all_gather(tokens, "head", axis=0, tiled=True)
    row_len = group_rows.shape[0]
    local_dim = w_qkv.shape[2]
    local_heads = local_dim // HEAD_DIM
    segment = segment_ids(lengths, row_len)[0]
    query_scale = HEAD_DIM ** (-0.5)
    projected = jnp.einsum("td,dce->tce", group_rows, w_qkv, preferred_element_type=jnp.float32)
    queries = ((projected[:, 0] + bias_qv[:, 0]) * query_scale).astype(jnp.bfloat16)
    key_rows = projected[:, 1].astype(jnp.bfloat16)
    value_rows = (projected[:, 2] + bias_qv[:, 1]).astype(jnp.bfloat16)
    block_rows = min(512, row_len)
    block_count = row_len // block_rows
    key_heads = key_rows.reshape(row_len, local_heads, HEAD_DIM)
    value_heads = value_rows.reshape(row_len, local_heads, HEAD_DIM)
    query_blocks = queries.reshape(block_count, block_rows, local_heads, HEAD_DIM)
    segment_blocks = segment.reshape(block_count, block_rows)

    def forward_block(block_items):
        query_part, segment_part = block_items
        scores = jnp.einsum(
            "qhe,khe->hqk", query_part, key_heads, preferred_element_type=jnp.float32
        )
        allowed = (segment_part[:, None] == segment[None, :])[None]
        scores = jnp.where(allowed, scores, -1e30)
        row_max = jnp.max(scores, axis=-1, keepdims=True)
        powers = jnp.exp(scores - row_max)
        row_total = jnp.sum(powers, axis=-1, keepdims=True)
        attn_probs = (powers / row_total).astype(jnp.bfloat16)
        output = jnp.einsum(
            "hqk,khe->qhe", attn_probs, value_heads, preferred_element_type=jnp.float32
        )
        return (output.astype(jnp.bfloat16), (row_max + jnp.log(row_total))[..., 0])

    attended, log_totals = lax.map(forward_block, (query_blocks, segment_blocks))
    attended = attended.reshape(row_len, local_dim)
    token_mixed = lax.all_to_all(attended, "head", split_axis=0, concat_axis=1, tiled=True)
    inputs = tokens.astype(jnp.float32)
    branch = jnp.dot(token_mixed, w_out, preferred_element_type=jnp.float32) + bias_out
    normed_one, norm_one_back = jax.vjp(layer_norm, inputs + branch, ln1_gain, ln1_bias)
    normed_low = normed_one.astype(jnp.bfloat16)
    hidden_pre = jnp.dot(normed_low, w_in, preferred_element_type=jnp.float32) + bias_in
    activated, gelu_back = jax.vjp(partial(jax.nn.gelu, approximate=False), hidden_pre)
    active_low = activated.astype(jnp.bfloat16)
    ffn_out = jnp.dot(active_low, w_down, preferred_element_type=jnp.float32) + bias_down
    normed_two, norm_two_back = jax.vjp(layer_norm, normed_one + ffn_out, ln2_gain, ln2_bias)
    term_logit = jnp.dot(normed_two, term_w, precision=highest) + term_bias[0]
    term_weight = jax.nn.softplus(term_logit)
    logit_grad = grad_term * jax.nn.sigmoid(term_logit)
    two_grad = grad_hidden + logit_grad[:, None] * term_w[None, :]
    term_w_local = jnp.dot(logit_grad, normed_two, precision=highest)
    term_bias_local = jnp.sum(logit_grad)
    resid_two_grad, gain_two_grad, shift_two_grad = norm_two_back(two_grad)
    ffn_grad = resid_two_grad.astype(jnp.bfloat16)
    down_local = jnp.einsum("tf,td->fd", active_low, ffn_grad, preferred_element_type=jnp.float32)
    bias_down_local = jnp.sum(ffn_grad.astype(jnp.float32), axis=0)
    active_grad = jnp.einsum("td,fd->tf", ffn_grad, w_down, preferred_element_type=jnp.float32)
    (pre_grad,) = gelu_back(active_grad)
    pre_low = pre_grad.astype(jnp.bfloat16)
    in_local = jnp.einsum("td,tf->df", normed_low, pre_low, preferred_element_type=jnp.float32)
    bias_in_local = jnp.sum(pre_low.astype(jnp.float32), axis=0)
    one_grad = resid_two_grad + jnp.einsum(
        "tf,df->td", pre_low, w_in, preferred_element_type=jnp.float32
    )
    resid_one_grad, gain_one_grad, shift_one_grad = norm_one_back(one_grad)
    branch_low = resid_one_grad.astype(jnp.bfloat16)
    out_local = jnp.einsum("te,td->ed", token_mixed, branch_low, preferred_element_type=jnp.float32)
    bias_out_local = jnp.sum(branch_low.astype(jnp.float32), axis=0)
    mixed_grad = jnp.einsum(
        "td,ed->te", branch_low, w_out, preferred_element_type=jnp.float32
    ).astype(jnp.bfloat16)
    head_grad = lax.all_to_all(mixed_grad, "head", split_axis=1, concat_axis=0, tiled=True)
    grad_blocks = head_grad.reshape(block_count, block_rows, local_heads, HEAD_DIM)

    def backward_block(totals_in, block_items):
        key_total, value_total = totals_in
        query_part, segment_part, grad_part, log_part = block_items
        scores = jnp.einsum(
            "qhe,khe->hqk", query_part, key_heads, preferred_element_type=jnp.float32
        )
        allowed = (segment_part[:, None] == segment[None, :])[None]
        attn_probs = jnp.exp(jnp.where(allowed, scores, -1e30) - log_part[..., None])
        value_total = value_total + jnp.einsum(
            "hqk,qhe->khe",
            attn_probs.astype(jnp.bfloat16),
            grad_part,
            preferred_element_type=jnp.float32,
        )
        prob_grad = jnp.einsum(
            "qhe,khe->hqk", grad_part, value_heads, preferred_element_type=jnp.float32
        )
        row_inner = jnp.sum(attn_probs * prob_grad, axis=-1, keepdims=True)
        score_grad = (attn_probs * (prob_grad - row_inner)).astype(jnp.bfloat16)
        query_grad = jnp.einsum(
            "hqk,khe->qhe", score_grad, key_heads, preferred_element_type=jnp.float32
        )
        key_total = key_total + jnp.einsum(
            "hqk,qhe->khe", score_grad, query_part, preferred_element_type=jnp.float32
        )
        return ((key_total, value_total), query_grad.astype(jnp.bfloat16))

    zero_heads = jnp.zeros((row_len, local_heads, HEAD_DIM), jnp.float32)
    (key_total, value_total), query_grads = lax.scan(
        backward_block,
        (zero_heads, zero_heads),
        (query_blocks, segment_blocks, grad_blocks, log_totals),
    )
    raw_grad = jnp.stack(
        [
            query_grads.reshape(row_len, local_dim) * query_scale,
            key_total.reshape(row_len, local_dim).astype(jnp.bfloat16),
            value_total.reshape(row_len, local_dim).astype(jnp.bfloat16),
        ],
        axis=1,
    )
    qkv_local = jnp.einsum("td,tce->dce", group_rows, raw_grad, preferred_element_type=jnp.float32)
    bias_qv_local = jnp.stack(
        [
            jnp.sum(raw_grad[:, 0].astype(jnp.float32), axis=0),
            jnp.sum(raw_grad[:, 2].astype(jnp.float32), axis=0),
        ],
        axis=1,
    )
    grad_tokens = resid_one_grad + lax.psum_scatter(
        jnp.einsum("tce,dce->td", raw_grad, w_qkv, preferred_element_type=jnp.float32).astype(
            jnp.bfloat16
        ),
        "head",
        scatter_dimension=0,
        tiled=True,
    ).astype(jnp.float32)
    core_index = lax.axis_index("head")
    bias_full = lax.dynamic_update_slice(
        jnp.zeros((MODEL_DIM, 2), jnp.float32),
        bias_qv_local,
        (core_index * local_dim, jnp.int32(0)),
    )
    summed = (
        lax.psum_scatter(out_local, ("dp", "head"), scatter_dimension=0, tiled=True),
        lax.psum_scatter(bias_out_local, ("dp", "head"), scatter_dimension=0, tiled=True),
        lax.psum_scatter(gain_one_grad, ("dp", "head"), scatter_dimension=0, tiled=True),
        lax.psum_scatter(shift_one_grad, ("dp", "head"), scatter_dimension=0, tiled=True),
        lax.psum_scatter(in_local, ("dp", "head"), scatter_dimension=0, tiled=True),
        lax.psum_scatter(bias_in_local, ("dp", "head"), scatter_dimension=0, tiled=True),
        lax.psum_scatter(down_local, ("dp", "head"), scatter_dimension=0, tiled=True),
        lax.psum_scatter(bias_down_local, ("dp", "head"), scatter_dimension=0, tiled=True),
        lax.psum_scatter(gain_two_grad, ("dp", "head"), scatter_dimension=0, tiled=True),
        lax.psum_scatter(shift_two_grad, ("dp", "head"), scatter_dimension=0, tiled=True),
        lax.psum_scatter(term_w_local, ("dp", "head"), scatter_dimension=0, tiled=True),
        lax.psum_scatter(bias_full, ("dp", "head"), scatter_dimension=0, tiled=True),
    )
    qkv_summed = lax.psum_scatter(qkv_local, "dp", scatter_dimension=0, tiled=True)
    term_bias_total = lax.psum(term_bias_local, ("dp", "head")).reshape(1)
    return (
        normed_two.astype(jnp.bfloat16),
        term_weight,
        grad_tokens,
        qkv_summed,
        summed[11],
        summed[0],
        summed[1],
        summed[2],
        summed[3],
        summed[4],
        summed[5],
        summed[6],
        summed[7],
        summed[8],
        summed[9],
        summed[10],
        term_bias_total,
    )


def solution(mesh):
    return jax.shard_map(
        shards,
        mesh=mesh,
        in_specs=(
            P(("dp", "head"), None),
            P("dp", None),
            P(None, None, "head"),
            P("head", None),
            P(),
            P(),
            P(),
            P(),
            P(),
            P(),
            P(),
            P(),
            P(),
            P(),
            P(),
            P(),
            P(("dp", "head"), None),
            P(("dp", "head")),
        ),
        out_specs=(
            P(("dp", "head"), None),
            P(("dp", "head")),
            P(("dp", "head"), None),
            P("dp", None, "head"),
            P(("dp", "head"), None),
            P(("dp", "head"), None),
            P(("dp", "head")),
            P(("dp", "head")),
            P(("dp", "head")),
            P(("dp", "head"), None),
            P(("dp", "head")),
            P(("dp", "head"), None),
            P(("dp", "head")),
            P(("dp", "head")),
            P(("dp", "head")),
            P(("dp", "head")),
            P(),
        ),
        check_vma=False,
    )
```

profile of v0, /device:TPU:0, one launch (start us, length us, event | category | flops | bytes accessed | tf_op | source)
XLA Modules:
  0.0 1293.7 jit_solution(5693191650572222730)
XLA Ops:
  46.0 154.2 %while.27 = (s32[]{:T(128)}, bf16[4,512,6,64]{1,3,2,0:T(8,128)(2,1)}, f32[4,6,512]{2,1,0:T(8,128)}, s32[4,512]{1,0:T(4,128)S(1)}, s32[1,2048]{1,0:T(1,128)S(1)},...) while((s32[]{:T(128)}, ...), condition=%wide.region_5.6_spmd, body=%wide.region_2.5_spmd.sunk | while | flops 1668477952 | bytes 83742304 | solution.py:81
  46.8 13.6 %select_reduce_fusion.2 = (f32[6,512]{1,0:T(8,128)S(1)}, f32[6,512,2048]{2,1,0:T(8,128)}) fusion(pred[512,2048]{1,0:T(8,128)(4,1)S(1)} %broadcast_compare_fusion.4, bf16[2048,6,64]{0,2,1:T(8,128)(2,1)} %get-tuple-element.495, bf16[4,512,6,64]{1,3,2,0:T(8,128)(2,1)} %get-tuple-element.494, s32[]{:T(128)} %get-tuple-element.480), kind=kOutput, calls=%fused_computation.2.clone.1 | convolution fusion | flops 817886208 | bytes 28193280 | tf_op jit(solution)/shard_map/while/body/eval_jaxpr/qhe,khe->hqk/dot_general | solution.py:67
  60.5 11.7 fusion.125
  72.8 11.9 fusion.126
  85.3 13.6 %select_reduce_fusion.2 = (f32[6,512]{1,0:T(8,128)S(1)}, f32[6,512,2048]{2,1,0:T(8,128)}) fusion(pred[512,2048]{1,0:T(8,128)(4,1)S(1)} %broadcast_compare_fusion.4, bf16[2048,6,64]{0,2,1:T(8,128)(2,1)} %get-tuple-element.495, bf16[4,512,6,64]{1,3,2,0:T(8,128)(2,1)} %get-tuple-element.494, s32[]{:T(128)} %get-tuple-element.480), kind=kOutput, calls=%fused_computation.2.clone.1 | convolution fusion | flops 817886208 | bytes 28193280 | tf_op jit(solution)/shard_map/while/body/eval_jaxpr/qhe,khe->hqk/dot_general | solution.py:67
  99.0 11.7 fusion.125
  111.3 11.9 fusion.126
  123.8 13.6 %select_reduce_fusion.2 = (f32[6,512]{1,0:T(8,128)S(1)}, f32[6,512,2048]{2,1,0:T(8,128)}) fusion(pred[512,2048]{1,0:T(8,128)(4,1)S(1)} %broadcast_compare_fusion.4, bf16[2048,6,64]{0,2,1:T(8,128)(2,1)} %get-tuple-element.495, bf16[4,512,6,64]{1,3,2,0:T(8,128)(2,1)} %get-tuple-element.494, s32[]{:T(128)} %get-tuple-element.480), kind=kOutput, calls=%fused_computation.2.clone.1 | convolution fusion | flops 817886208 | bytes 28193280 | tf_op jit(solution)/shard_map/while/body/eval_jaxpr/qhe,khe->hqk/dot_general | solution.py:67
  137.5 11.7 fusion.125
  149.8 11.9 fusion.126
  162.3 13.6 %select_reduce_fusion.2 = (f32[6,512]{1,0:T(8,128)S(1)}, f32[6,512,2048]{2,1,0:T(8,128)}) fusion(pred[512,2048]{1,0:T(8,128)(4,1)S(1)} %broadcast_compare_fusion.4, bf16[2048,6,64]{0,2,1:T(8,128)(2,1)} %get-tuple-element.495, bf16[4,512,6,64]{1,3,2,0:T(8,128)(2,1)} %get-tuple-element.494, s32[]{:T(128)} %get-tuple-element.480), kind=kOutput, calls=%fused_computation.2.clone.1 | convolution fusion | flops 817886208 | bytes 28193280 | tf_op jit(solution)/shard_map/while/body/eval_jaxpr/qhe,khe->hqk/dot_general | solution.py:67
  176.0 11.7 fusion.125
  188.3 11.9 fusion.126
  221.0 35.9 %multiply_convert_fusion.1 = (bf16[1024,3072]{1,0:T(8,128)(2,1)}, f32[1024,3072]{1,0:T(8,128)}, f32[1024,3072]{1,0:T(8,128)}) fusion(f32[3072]{0:T(1024)S(1)} %copy-done.49, bf16[768,3072]{1,0:T(8,128)(2,1)S(1)} %bitcast.168, f32[1024,768]{0,1:T(8,128)S(1)} %get-tuple-element.340, f32[768]{0:T(1024)S(1)} %copy-done.52, f32[768]{0:T(1024)S(1)} %copy-done.41, ...), kind=kOutput, calls=%fused_computation.51 | convolution fusion | flops 5043388416 | bytes 39348224 | tf_op jit(solution)/shard_map/dot_general | solution.py:88
  276.5 18.1 %convert_reduce_fusion = (f32[3072]{0:T(1024)}, bf16[1024,3072]{1,0:T(8,128)(2,1)}) fusion(f32[1024,3072]{1,0:T(8,128)} %get-tuple-element.330, bf16[1024,768]{0,1:T(8,128)(2,1)S(1)} %get-tuple-element.320, bf16[3072,768]{1,0:T(8,128)(2,1)} %param.32, f32[1024,3072]{1,0:T(8,128)} %get-tuple-element.341, f32[3072]{0:T(1024)S(1)} %copy-done.49), kind=kOutput, calls=%fused_computation.49 | convolution fusion | flops 4885312512 | bytes 37773312 | tf_op jit(solution)/shard_map/td,fd->tf/dot_general | solution.py:103
  294.5 10.8 multiply_reduce_fusion.2
  322.4 344.7 %while.28 = (s32[]{:T(128)}, f32[2048,6,64]{0,2,1:T(8,128)}, f32[2048,6,64]{0,2,1:T(8,128)}, bf16[4,512,6,64]{1,3,2,0:T(8,128)(2,1)}, bf16[4,512,6,64]{1,3,2,0:T...) while((s32[]{:T(128)}, f32[2048,6,64]{0,2,1:T(8,128)}, ...), condition=%wide.region_16.17_spmd.clone, body=%wide.region_14.16_spmd.clone.sunk | while | flops 4106417152 | bytes 212308624 | solution.py:149
  322.8 13.3 %fusion.136 = f32[6,512,2048]{2,1,0:T(8,128)} fusion(bf16[2048,6,64]{0,2,1:T(8,128)(2,1)} %get-tuple-element.531, bf16[4,512,6,64]{1,3,2,0:T(8,128)(2,1)} %get-tuple-element.528, s32[]{:T(128)} %get-tuple-element.511), kind=kOutput, calls=%fused_computation.34.clone.1 | convolution fusion | flops 805306368 | bytes 27132416 | tf_op jit(solution)/shard_map/while/body/eval_jaxpr/qhe,khe->hqk/dot_general | solution.py:124
  338.2 17.3 %multiply_reduce_fusion.8 = (f32[6,512]{1,0:T(8,128)S(1)}, f32[6,512,2048]{2,1,0:T(8,128)}) fusion(f32[6,512,2048]{2,1,0:T(8,128)} %fusion.136, f32[6,512]{1,0:T(8,128)S(1)} %dynamic-slice_bitcast_fusion.2, pred[512,2048]{1,0:T(8,128)(4,1)S(1)} %broadcast_compare_fusion.5, bf16[2048,6,64]{0,2,1:T(8,128)(2,1)} %get-tuple-element.534, ...), kind=kOutput, calls=%fused_computation.17.clone.1 | convolution fusion | flops 830469120 | bytes 53371392 | tf_op jit(solution)/shard_map/while/body/eval_jaxpr/qhe,khe->hqk/dot_general | solution.py:135
  355.6 21.1 %multiply_convert_fusion.3 = bf16[6,512,2048]{2,1,0:T(8,128)(2,1)} fusion(f32[6,512,2048]{2,1,0:T(8,128)} %get-tuple-element.469, f32[6,512,2048]{2,1,0:T(8,128)} %fusion.136, f32[6,512]{1,0:T(8,128)S(1)} %get-tuple-element.470, f32[6,512]{1,0:T(8,128)S(1)} %dynamic-slice_bitcast_fusion.2, pred[512,2048]{1,0:T(8,128)(4,1)S(1)} %broadcast_compare_fusion.5), kind=kLoop, calls=%fused_computation.16.clone.1 | loop fusion | flops 31457280 | bytes 63987712 | tf_op jit(solution)/shard_map/while/body/eval_jaxpr/convert_element_type | solution.py:139
  385.4 9.7 fusion.137
  395.0 12.4 bitcast_add_fusion.5
  407.5 13.3 %fusion.136 = f32[6,512,2048]{2,1,0:T(8,128)} fusion(bf16[2048,6,64]{0,2,1:T(8,128)(2,1)} %get-tuple-element.531, bf16[4,512,6,64]{1,3,2,0:T(8,128)(2,1)} %get-tuple-element.528, s32[]{:T(128)} %get-tuple-element.511), kind=kOutput, calls=%fused_computation.34.clone.1 | convolution fusion | flops 805306368 | bytes 27132416 | tf_op jit(solution)/shard_map/while/body/eval_jaxpr/qhe,khe->hqk/dot_general | solution.py:124
  422.9 17.4 %multiply_reduce_fusion.8 = (f32[6,512]{1,0:T(8,128)S(1)}, f32[6,512,2048]{2,1,0:T(8,128)}) fusion(f32[6,512,2048]{2,1,0:T(8,128)} %fusion.136, f32[6,512]{1,0:T(8,128)S(1)} %dynamic-slice_bitcast_fusion.2, pred[512,2048]{1,0:T(8,128)(4,1)S(1)} %broadcast_compare_fusion.5, bf16[2048,6,64]{0,2,1:T(8,128)(2,1)} %get-tuple-element.534, ...), kind=kOutput, calls=%fused_computation.17.clone.1 | convolution fusion | flops 830469120 | bytes 53371392 | tf_op jit(solution)/shard_map/while/body/eval_jaxpr/qhe,khe->hqk/dot_general | solution.py:135
  440.2 21.1 %multiply_convert_fusion.3 = bf16[6,512,2048]{2,1,0:T(8,128)(2,1)} fusion(f32[6,512,2048]{2,1,0:T(8,128)} %get-tuple-element.469, f32[6,512,2048]{2,1,0:T(8,128)} %fusion.136, f32[6,512]{1,0:T(8,128)S(1)} %get-tuple-element.470, f32[6,512]{1,0:T(8,128)S(1)} %dynamic-slice_bitcast_fusion.2, pred[512,2048]{1,0:T(8,128)(4,1)S(1)} %broadcast_compare_fusion.5), kind=kLoop, calls=%fused_computation.16.clone.1 | loop fusion | flops 31457280 | bytes 63987712 | tf_op jit(solution)/shard_map/while/body/eval_jaxpr/convert_element_type | solution.py:139
  461.4 9.6 bitcast_add_fusion.4
  470.9 9.7 fusion.137
  480.6 13.4 %bitcast_add_fusion.5 = f32[2048,6,64]{0,2,1:T(8,128)} fusion(f32[2048,6,64]{0,2,1:T(8,128)} %get-tuple-element.513, f32[6,512,2048]{2,1,0:T(8,128)} %fusion.136, f32[6,512]{1,0:T(8,128)S(1)} %dynamic-slice_bitcast_fusion.2, pred[512,2048]{1,0:T(8,128)(4,1)S(1)} %broadcast_compare_fusion.5, pred[]{:T(512)S(6)} %compare.3, ...), kind=kOutput, calls=%fused_computation.24.clone.1 | convolution fusion | flops 825753600 | bytes 32911872 | tf_op jit(solution)/shard_map/while/body/eval_jaxpr/hqk,qhe->khe/dot_general | solution.py:129
  494.0 13.3 %fusion.136 = f32[6,512,2048]{2,1,0:T(8,128)} fusion(bf16[2048,6,64]{0,2,1:T(8,128)(2,1)} %get-tuple-element.531, bf16[4,512,6,64]{1,3,2,0:T(8,128)(2,1)} %get-tuple-element.528, s32[]{:T(128)} %get-tuple-element.511), kind=kOutput, calls=%fused_computation.34.clone.1 | convolution fusion | flops 805306368 | bytes 27132416 | tf_op jit(solution)/shard_map/while/body/eval_jaxpr/qhe,khe->hqk/dot_general | solution.py:124
  509.4 17.4 %multiply_reduce_fusion.8 = (f32[6,512]{1,0:T(8,128)S(1)}, f32[6,512,2048]{2,1,0:T(8,128)}) fusion(f32[6,512,2048]{2,1,0:T(8,128)} %fusion.136, f32[6,512]{1,0:T(8,128)S(1)} %dynamic-slice_bitcast_fusion.2, pred[512,2048]{1,0:T(8,128)(4,1)S(1)} %broadcast_compare_fusion.5, bf16[2048,6,64]{0,2,1:T(8,128)(2,1)} %get-tuple-element.534, ...), kind=kOutput, calls=%fused_computation.17.clone.1 | convolution fusion | flops 830469120 | bytes 53371392 | tf_op jit(solution)/shard_map/while/body/eval_jaxpr/qhe,khe->hqk/dot_general | solution.py:135
  526.7 21.1 %multiply_convert_fusion.3 = bf16[6,512,2048]{2,1,0:T(8,128)(2,1)} fusion(f32[6,512,2048]{2,1,0:T(8,128)} %get-tuple-element.469, f32[6,512,2048]{2,1,0:T(8,128)} %fusion.136, f32[6,512]{1,0:T(8,128)S(1)} %get-tuple-element.470, f32[6,512]{1,0:T(8,128)S(1)} %dynamic-slice_bitcast_fusion.2, pred[512,2048]{1,0:T(8,128)(4,1)S(1)} %broadcast_compare_fusion.5), kind=kLoop, calls=%fused_computation.16.clone.1 | loop fusion | flops 31457280 | bytes 63987712 | tf_op jit(solution)/shard_map/while/body/eval_jaxpr/convert_element_type | solution.py:139
  547.9 9.6 bitcast_add_fusion.4
  557.4 9.7 fusion.137
  567.1 13.4 %bitcast_add_fusion.5 = f32[2048,6,64]{0,2,1:T(8,128)} fusion(f32[2048,6,64]{0,2,1:T(8,128)} %get-tuple-element.513, f32[6,512,2048]{2,1,0:T(8,128)} %fusion.136, f32[6,512]{1,0:T(8,128)S(1)} %dynamic-slice_bitcast_fusion.2, pred[512,2048]{1,0:T(8,128)(4,1)S(1)} %broadcast_compare_fusion.5, pred[]{:T(512)S(6)} %compare.3, ...), kind=kOutput, calls=%fused_computation.24.clone.1 | convolution fusion | flops 825753600 | bytes 32911872 | tf_op jit(solution)/shard_map/while/body/eval_jaxpr/hqk,qhe->khe/dot_general | solution.py:129
  580.5 13.3 %fusion.136 = f32[6,512,2048]{2,1,0:T(8,128)} fusion(bf16[2048,6,64]{0,2,1:T(8,128)(2,1)} %get-tuple-element.531, bf16[4,512,6,64]{1,3,2,0:T(8,128)(2,1)} %get-tuple-element.528, s32[]{:T(128)} %get-tuple-element.511), kind=kOutput, calls=%fused_computation.34.clone.1 | convolution fusion | flops 805306368 | bytes 27132416 | tf_op jit(solution)/shard_map/while/body/eval_jaxpr/qhe,khe->hqk/dot_general | solution.py:124
  595.9 17.4 %multiply_reduce_fusion.8 = (f32[6,512]{1,0:T(8,128)S(1)}, f32[6,512,2048]{2,1,0:T(8,128)}) fusion(f32[6,512,2048]{2,1,0:T(8,128)} %fusion.136, f32[6,512]{1,0:T(8,128)S(1)} %dynamic-slice_bitcast_fusion.2, pred[512,2048]{1,0:T(8,128)(4,1)S(1)} %broadcast_compare_fusion.5, bf16[2048,6,64]{0,2,1:T(8,128)(2,1)} %get-tuple-element.534, ...), kind=kOutput, calls=%fused_computation.17.clone.1 | convolution fusion | flops 830469120 | bytes 53371392 | tf_op jit(solution)/shard_map/while/body/eval_jaxpr/qhe,khe->hqk/dot_general | solution.py:135
  613.2 21.1 %multiply_convert_fusion.3 = bf16[6,512,2048]{2,1,0:T(8,128)(2,1)} fusion(f32[6,512,2048]{2,1,0:T(8,128)} %get-tuple-element.469, f32[6,512,2048]{2,1,0:T(8,128)} %fusion.136, f32[6,512]{1,0:T(8,128)S(1)} %get-tuple-element.470, f32[6,512]{1,0:T(8,128)S(1)} %dynamic-slice_bitcast_fusion.2, pred[512,2048]{1,0:T(8,128)(4,1)S(1)} %broadcast_compare_fusion.5), kind=kLoop, calls=%fused_computation.16.clone.1 | loop fusion | flops 31457280 | bytes 63987712 | tf_op jit(solution)/shard_map/while/body/eval_jaxpr/convert_element_type | solution.py:139
  634.4 9.6 bitcast_add_fusion.4
  644.0 9.7 fusion.137
  653.6 13.4 %bitcast_add_fusion.5 = f32[2048,6,64]{0,2,1:T(8,128)} fusion(f32[2048,6,64]{0,2,1:T(8,128)} %get-tuple-element.513, f32[6,512,2048]{2,1,0:T(8,128)} %fusion.136, f32[6,512]{1,0:T(8,128)S(1)} %dynamic-slice_bitcast_fusion.2, pred[512,2048]{1,0:T(8,128)(4,1)S(1)} %broadcast_compare_fusion.5, pred[]{:T(512)S(6)} %compare.3, ...), kind=kOutput, calls=%fused_computation.24.clone.1 | convolution fusion | flops 825753600 | bytes 32911872 | tf_op jit(solution)/shard_map/while/body/eval_jaxpr/hqk,qhe->khe/dot_general | solution.py:129
  716.6 10.1 fusion.80
  727.4 10.6 fusion.68
  745.5 42.4 %all-reduce.10 = (f32[768,2]{0,1:T(2,128)S(1)}, f32[768]{0:T(1024)S(1)}, f32[768]{0:T(1024)S(1)}, f32[768]{0:T(1024)S(1)}, f32[3072]{0:T(1024)S(1)}, /*index=5*/...) all-reduce(f32[768,2]{0,1:T(2,128)S(1)} %maximum_dynamic-update-sli, ...), channel_id=4, replica_groups=mesh['dp'=16,'head'=2] {'dp','head'}, use_global_device_ids=true, to_apply=%region_21.22.clone | all-reduce | flops 9985 | bytes 79880
  794.8 90.0 %all-reduce.13.cloned.1.call-done = f32[768,3,384]{2,1,0:T(4,128)} async-done(((f32[768,3,384]{2,1,0:T(4,128)}), f32[768,3,384]{2,1,0:T(4,128)}) %all-reduce.13.cloned.1.call-update) | async-done | bytes 3538960
  886.6 11.2 reduce-scatter.6.cloned.1.call-done
  906.1 97.6 %reduce-scatter.8.cloned.1.call-done = f32[24,768]{1,0:T(8,128)} async-done(((f32[768,768]{1,0:T(8,128)}), f32[24,768]{1,0:T(8,128)}) %reduce-scatter.8.cloned.1.call-update) | async-done | bytes 73744 | tf_op jit(solution)/shard_map/reduce_scatter | solution.py:185
  1003.7 142.0 %reduce-scatter.12.cloned.1.call-done = f32[96,768]{1,0:T(8,128)} async-done(((f32[3072,768]{1,0:T(8,128)}), f32[96,768]{1,0:T(8,128)}) %reduce-scatter.12.cloned.1.call-update) | async-done | bytes 294928 | tf_op jit(solution)/shard_map/reduce_scatter | solution.py:191
  1145.7 141.0 %reduce-scatter.10.cloned.1.call-done = f32[24,3072]{1,0:T(8,128)} async-done(((f32[768,3072]{1,0:T(8,128)}), f32[24,3072]{1,0:T(8,128)}) %reduce-scatter.10.cloned.1.call-update) | async-done | bytes 294928 | tf_op jit(solution)/shard_map/reduce_scatter | solution.py:189
  (241 shorter events, 190.9 us)
Async XLA Ops:
  7.2 17.3 %copy-start = (bf16[768,3,384]{2,0,1:T(8,128)(2,1)S(1)}, bf16[768,3,384]{2,0,1:T(8,128)(2,1)}, u32[]{:S(2)}) copy-start(bf16[768,3,384]{2,0,1:T(8,128)(2,1)} %param.24) | copy-start | bytes 5308420
  7.2 3.5 copy-start.46
  7.2 3.7 copy-start.54
  7.2 4.0 copy-start.29
  7.2 17.2 %all-gather.2.cloned.1.call-start = ((), (), s32[]{:S(2)}) async-start(), calls=%async_computation.6 | async-start | bytes 4718592 | tf_op jit(solution)/shard_map/all_gather | solution.py:48
  8.0 876.9 %all-reduce.13.cloned.1.call-start = ((), (), s32[]{:S(2)}) async-start(), calls=%async_computation.11 | async-start | bytes 9437184
  40.1 4.3 copy-start.8
  200.2 9.2 copy-start.2
  200.2 9.2 copy-start.14
  200.2 9.2 copy-start.20
  209.4 7.2 copy-start.11
  209.4 7.2 copy-start.47
  209.4 7.2 copy-start.50
  216.6 3.0 slice-start.2
  216.7 3.4 slice-start.3
  216.7 40.3 %slice-start = ((s8[4718592]{0:T(1024)(128)(4,1)}), s8[4194304]{0:T(1024)(128)(4,1)S(1)}, s32[]{:S(2)}) async-start(s8[4718592]{0:T(1024)(128)(4,1)} %bitcast.165), calls=%async_computation.12 | async-start | bytes 8388608
  218.4 86.9 %copy-start.6 = (f32[1024,768]{0,1:T(8,128)}, f32[1024,768]{0,1:T(8,128)S(1)}, u32[]{:S(2)}) copy-start(f32[1024,768]{0,1:T(8,128)S(1)} %get-tuple-element.340) | copy-start | bytes 9437188
  218.4 2.6 copy-start.49
  218.4 2.6 copy-start.52
  218.4 86.9 %copy-start.31 = (f32[1024]{0:T(1024)}, f32[1024]{0:T(1024)S(1)}, u32[]{:S(2)}) copy-start(f32[1024]{0:T(1024)S(1)} %broadcast_multiply_fusion.2) | copy-start | bytes 12292
  221.0 84.3 %copy-start.37 = (f32[1024]{0:T(1024)}, f32[1024]{0:T(1024)S(1)}, u32[]{:S(2)}) copy-start(f32[1024]{0:T(1024)S(1)} %fusion.64) | copy-start | bytes 12292
  221.0 35.9 %slice-start.1 = ((s8[4718592]{0:T(1024)(128)(4,1)}), s8[524288]{0:T(1024)(128)(4,1)S(1)}, s32[]{:S(2)}) async-start(s8[4718592]{0:T(1024)(128)(4,1)} %bitcast.165), calls=%async_computation.13 | async-start | bytes 1048576
  221.0 35.9 %copy-start.51 = (f32[768]{0:T(1024)S(1)}, f32[768]{0:T(1024)}, u32[]{:S(2)}) copy-start(f32[768]{0:T(1024)} %param.33) | copy-start | bytes 9220
  265.0 6.3 copy-start.1
  265.1 6.2 copy-start.16
  265.1 2.9 copy-start.43
  265.1 4.1 copy-start.4
  265.1 4.1 copy-start.30
  265.8 5.4 copy-start.18
  276.5 18.1 %copy-start.12 = (bf16[1024,768]{0,1:T(8,128)(2,1)}, bf16[1024,768]{0,1:T(8,128)(2,1)S(1)}, u32[]{:S(2)}) copy-start(bf16[1024,768]{0,1:T(8,128)(2,1)S(1)} %get-tuple-element.320) | copy-start | bytes 4718596
  306.1 3.6 copy-start.3
  306.1 3.5 copy-start.25
  307.1 2.6 copy-start.13
  318.2 4.2 copy-start.15
  667.2 3.3 copy-start.5
  703.2 194.5 %reduce-scatter.6.cloned.1.call-start = ((), (), s32[]{:S(2)}) async-start(), calls=%async_computation.7 | async-start | bytes 4718592 | tf_op jit(solution)/shard_map/reduce_scatter | solution.py:170
  711.5 292.1 %reduce-scatter.8.cloned.1.call-start = ((), (), s32[]{:S(2)}) async-start(), calls=%async_computation.8 | async-start | bytes 2433024 | tf_op jit(solution)/shard_map/reduce_scatter | solution.py:185
  716.5 429.2 %reduce-scatter.12.cloned.1.call-start = ((), (), s32[]{:S(2)}) async-start(), calls=%async_computation.10 | async-start | bytes 9732096 | tf_op jit(solution)/shard_map/reduce_scatter | solution.py:191
  726.8 559.9 %reduce-scatter.10.cloned.1.call-start = ((), (), s32[]{:S(2)}) async-start(), calls=%async_computation.9 | async-start | bytes 9732096 | tf_op jit(solution)/shard_map/reduce_scatter | solution.py:189
  738.1 7.3 copy-start.33
  738.2 7.3 copy-start.34
  738.2 7.3 copy-start.35
  738.2 7.3 copy-start.36
  738.2 7.3 copy-start.40
  738.2 7.3 copy-start.44
  738.2 7.3 copy-start.45
  740.4 51.6 %copy-start.9 = (bf16[1024,768]{0,1:T(8,128)(2,1)S(1)}, bf16[1024,768]{0,1:T(8,128)(2,1)}, u32[]{:S(2)}) copy-start(bf16[1024,768]{0,1:T(8,128)(2,1)} %get-tuple-element.337) | copy-start | bytes 4718596
  740.6 157.1 %copy-start.26 = (f32[1024]{0:T(1024)S(1)}, f32[1024]{0:T(1024)}, u32[]{:S(2)}) copy-start(f32[1024]{0:T(1024)} %copy-done.25) | copy-start | bytes 12292
  (18 other events, 28.2 us)
Sparse Core Ops, SparseCore 0:
  9.6 14.8 all-gather.1
  703.3 181.4 all-reduce.12
  887.7 9.9 reduce-scatter.5
  903.4 100.1 reduce-scatter.7
  1011.0 134.6 reduce-scatter.11
  1152.0 134.6 reduce-scatter.9
where the time goes:
time: 1300 us; the launch traced here: 1290 us
  waiting for transfers between devices  491 us (38%)
  matrix products  485 us (37%)
  other arithmetic  165 us (13%)
  local copies, waits for them, and re-layouts  82.5 us (6%)
  blocking collectives  52.6 us (4%)
  between operations  16.4 us (1%)
    reduce_scatter x1, waiting for transfers between devices, shards(): lax.psum_scatter(down_local, ('dp', 'head'), scatter_dimension=0, tiled=T...  142 us
    reduce_scatter x1, waiting for transfers between devices, shards(): lax.psum_scatter(in_local, ('dp', 'head'), scatter_dimension=0, tiled=True)  141 us
    reduce_scatter x1, waiting for transfers between devices, shards(): lax.psum_scatter(out_local, ('dp', 'head'), scatter_dimension=0, tiled=True)  97.6 us
    unnamed x7, waiting for transfers between devices  90.8 us
    convert_element_type x4, other arithmetic, backward_block(): score_grad = (attn_probs * (prob_grad - row_inner)).astype(jnp.bfloat16)  84.6 us
    dot_general x4, matrix products, backward_block(): jnp.einsum('qhe,khe->hqk', grad_part, value_heads, preferred_element_type...  69.4 us
    dot_general x4, matrix products, forward_block(): jnp.einsum('qhe,khe->hqk', query_part, key_heads, preferred_element_type=...  54.6 us
    dot_general x4, matrix products, backward_block(): jnp.einsum('qhe,khe->hqk', query_part, key_heads, preferred_element_type=...  53.2 us
  transfers between devices with their start and end apart: 6, of which 6 were waited for; matrix products, arithmetic and copies ran while one was open for 5% of the time, Pallas kernels for 0%

commit v1 on v0

v1 whole, which is shorter than its diff:
```python
from functools import partial

import jax
import jax.numpy as jnp
from jax import lax
from jax.experimental import pallas as pl
from jax.experimental.pallas import tpu as pltpu
from jax.sharding import PartitionSpec as P

HEAD_DIM = 64
LANES = 128
Q_ROWS = 256
WIDTHS = (2, 3, 4, 5, 6, 8, 10)
AXES = ("dp", "head")

f32 = jnp.float32
bf16 = jnp.bfloat16
highest = lax.Precision.HIGHEST
norm_eps = 1e-06
NT = (((1,), (1,)), ((), ()))
TN = (((0,), (0,)), ((), ()))


def layer_norm(resid, gain, shift):
    center = resid - jnp.mean(resid, axis=-1, keepdims=True)
    spread = jnp.mean(center * center, axis=-1, keepdims=True)
    return center * lax.rsqrt(spread + norm_eps) * gain + shift


def key_range(lengths_ref, first, rows, row_len):
    start = jnp.int32(0)
    low = jnp.int32(0)
    high = jnp.int32(row_len)
    for j in range(lengths_ref.shape[1]):
        end = start + lengths_ref[0, j]
        low = jnp.where(start <= first, start, low)
        high = jnp.where(end >= first + rows, jnp.minimum(high, end), high)
        start = end
    low_block = low // LANES
    count = (high + LANES - 1) // LANES - low_block
    return low_block, count


def by_width(lengths_ref, first, rows, row_len, body):
    blocks = row_len // LANES
    low_block, count = key_range(lengths_ref, first, rows, row_len)
    widths = sorted({min(w, blocks) for w in WIDTHS})
    below = 0
    for width in widths:

        @pl.when((count > below) & (count <= width))
        def _(width=width):
            begin = jnp.minimum(low_block, blocks - width)
            body(pl.multiple_of(begin * LANES, LANES), width * LANES)

        below = width


def attend_kernel(lengths_ref, q_ref, k_ref, v_ref, segc_ref, segr_ref, o_ref, log_ref, mask_ref, cols_ref):
    rows, local_dim = q_ref.shape
    row_len = k_ref.shape[0]
    first = pl.program_id(0) * rows
    lane = lax.broadcasted_iota(jnp.int32, (rows, LANES), 1)

    def body(begin, width):
        same = segc_ref[:, 0:1] == segr_ref[0:1, pl.ds(begin, width)]
        mask_ref[:, :width] = jnp.where(same, 0.0, -1e30)

        def pair_step(pair, carry):
            cols = pl.ds(pl.multiple_of(pair * LANES, LANES), LANES)
            q_pair = q_ref[:, cols]
            k_pair = k_ref[pl.ds(begin, width), cols]
            v_pair = v_ref[pl.ds(begin, width), cols]
            outs = []
            for h in range(2):
                mine = (lane // HEAD_DIM) == h
                q_one = jnp.where(mine, q_pair, jnp.zeros_like(q_pair))
                scores = lax.dot_general(q_one, k_pair, NT, preferred_element_type=f32)
                scores = scores + mask_ref[:, :width]
                row_max = jnp.max(scores, axis=1, keepdims=True)
                powers = jnp.exp(scores - row_max)
                total = jnp.sum(powers, axis=1, keepdims=True)
                probs = (powers * (1.0 / total)).astype(bf16)
                outs.append(jnp.dot(probs, v_pair, preferred_element_type=f32))
                log_total = row_max + jnp.log(total)
                cols_ref[...] = jnp.where(lane == 2 * pair + h, log_total, cols_ref[...])
            o_ref[:, cols] = jnp.where(lane < HEAD_DIM, outs[0], outs[1]).astype(bf16)
            return carry

        lax.fori_loop(0, local_dim // LANES, pair_step, 0)

    by_width(lengths_ref, first, rows, row_len, body)
    log_ref[...] = cols_ref[...].T[: log_ref.shape[0]]


def attend(lengths, queries, key_rows, value_rows, seg_col, seg_row):
    row_len, local_dim = queries.shape
    rows = min(Q_ROWS, row_len)
    whole = pl.BlockSpec((row_len, local_dim), lambda i, n: (0, 0))
    block = pl.BlockSpec((rows, local_dim), lambda i, n: (i, 0))
    return pl.pallas_call(
        attend_kernel,
        grid_spec=pltpu.PrefetchScalarGridSpec(
            num_scalar_prefetch=1,
            grid=(row_len // rows,),
            in_specs=[
                block,
                whole,
                whole,
                pl.BlockSpec((rows, LANES), lambda i, n: (i, 0)),
                pl.BlockSpec((8, row_len), lambda i, n: (0, 0)),
            ],
            out_specs=[block, pl.BlockSpec((8, rows), lambda i, n: (0, i))],
            scratch_shapes=[
                pltpu.VMEM((rows, max(WIDTHS) * LANES), f32),
                pltpu.VMEM((rows, LANES), f32),
            ],
        ),
        out_shape=[
            jax.ShapeDtypeStruct((row_len, local_dim), bf16),
            jax.ShapeDtypeStruct((8, row_len), f32),
        ],
        compiler_params=pltpu.CompilerParams(vmem_limit_bytes=48 * 2**20),
        cost_estimate=pl.CostEstimate(flops=20_000_000_000, bytes_accessed=8_000_000, transcendentals=0),
    )(lengths, queries, key_rows, value_rows, seg_col, seg_row)


def attend_back_kernel(
    lengths_ref, q_ref, k_ref, v_ref, g_ref, log_ref, segc_ref, segr_ref, raw_ref, sums_ref, mask_ref, dk_ref, dv_ref
):
    rows, local_dim = q_ref.shape
    row_len = k_ref.shape[0]
    step = pl.program_id(0)
    first = step * rows
    lane = lax.broadcasted_iota(jnp.int32, (rows, LANES), 1)

    @pl.when(step == 0)
    def _():
        dk_ref[...] = jnp.zeros_like(dk_ref)
        dv_ref[...] = jnp.zeros_like(dv_ref)

    def body(begin, width):
        keys = pl.ds(begin, width)
        same = segc_ref[keys, 0:1] == segr_ref[0:1, :]
        mask_ref[:width, :] = jnp.where(same, 0.0, -1e30)

        def pair_step(pair, carry):
            cols = pl.ds(pl.multiple_of(pair * LANES, LANES), LANES)
            q_pair, g_pair = q_ref[:, cols], g_ref[:, cols]
            k_pair, v_pair = k_ref[keys, cols], v_ref[keys, cols]
            dq = []
            dk = dv = None
            for h in range(2):
                mine = (lane // HEAD_DIM) == h
                q_one = jnp.where(mine, q_pair, jnp.zeros_like(q_pair))
                g_one = jnp.where(mine, g_pair, jnp.zeros_like(g_pair))
                scores = lax.dot_general(k_pair, q_one, NT, preferred_element_type=f32)
                probs = jnp.exp(scores + mask_ref[:width, :] - log_ref[pl.ds(2 * pair + h, 1), :])
                dv_one = jnp.dot(probs.astype(bf16), g_one, preferred_element_type=f32)
                prob_grad = lax.dot_general(v_pair, g_one, NT, preferred_element_type=f32)
                inner = jnp.sum(probs * prob_grad, axis=0, keepdims=True)
                score_grad = (probs * (prob_grad - inner)).astype(bf16)
                dk_one = jnp.dot(score_grad, q_one, preferred_element_type=f32)
                dq.append(lax.dot_general(score_grad, k_pair, TN, preferred_element_type=f32))
                dk = dk_one if dk is None else dk + dk_one
                dv = dv_one if dv is None else dv + dv_one
            dk_ref[keys, cols] += dk
            dv_ref[keys, cols] += dv
            dq_low = jnp.where(lane < HEAD_DIM, dq[0], dq[1]).astype(bf16)
            raw_ref[pl.ds(pl.multiple_of(first, rows), rows), cols] = dq_low * jnp.asarray(HEAD_DIM**-0.5, bf16)
            return carry

        lax.fori_loop(0, local_dim // LANES, pair_step, 0)

    by_width(lengths_ref, first, rows, row_len, body)

    @pl.when(step == pl.num_programs(0) - 1)
    def _():
        raw_ref[:, local_dim : 2 * local_dim] = dk_ref[...].astype(bf16)
        raw_ref[:, 2 * local_dim :] = dv_ref[...].astype(bf16)
        sums_ref[...] = jnp.sum(raw_ref[...].astype(f32), axis=0, keepdims=True)


def attend_back(lengths, queries, key_rows, value_rows, grads, logs, seg_col, seg_row):
    row_len, local_dim = queries.shape
    rows = min(Q_ROWS, row_len)
    whole = pl.BlockSpec((row_len, local_dim), lambda i, n: (0, 0))
    block = pl.BlockSpec((rows, local_dim), lambda i, n: (i, 0))
    return pl.pallas_call(
        attend_back_kernel,
        grid_spec=pltpu.PrefetchScalarGridSpec(
            num_scalar_prefetch=1,
            grid=(row_len // rows,),
            in_specs=[
                block,
                whole,
                whole,
                block,
                pl.BlockSpec((8, rows), lambda i, n: (0, i)),
                pl.BlockSpec((row_len, LANES), lambda i, n: (0, 0)),
                pl.BlockSpec((8, rows), lambda i, n: (0, i)),
            ],
            out_specs=[
                pl.BlockSpec((row_len, 3 * local_dim), lambda i, n: (0, 0)),
                pl.BlockSpec((1, 3 * local_dim), lambda i, n: (0, 0)),
            ],
            scratch_shapes=[
                pltpu.VMEM((max(WIDTHS) * LANES, rows), f32),
                pltpu.VMEM((row_len, local_dim), f32),
                pltpu.VMEM((row_len, local_dim), f32),
            ],
        ),
        out_shape=[
            jax.ShapeDtypeStruct((row_len, 3 * local_dim), bf16),
            jax.ShapeDtypeStruct((1, 3 * local_dim), f32),
        ],
        compiler_params=pltpu.CompilerParams(vmem_limit_bytes=56 * 2**20),
        cost_estimate=pl.CostEstimate(flops=40_000_000_000, bytes_accessed=12_000_000, transcendentals=0),
    )(lengths, queries, key_rows, value_rows, grads, logs, seg_col, seg_row)


def take(array, index, axis=0):
    return lax.dynamic_index_in_dim(array, index, axis, keepdims=False)


class Links:
    def __init__(self, n_dp):
        self.n_dp = n_dp
        self.bits = n_dp.bit_length() - 1
        self.dp = lax.axis_index("dp")
        self.head = lax.axis_index("head")

    def bit(self, which):
        return (self.dp >> which) & 1

    def permute(self, array, partner):
        pairs = []
        for d in range(self.n_dp):
            for h in range(2):
                to_d, to_h = partner(d, h)
                pairs.append((2 * d + h, 2 * to_d + to_h))
        return lax.ppermute(array, AXES, pairs)

    def swap_head(self, array):
        return self.permute(array, lambda d, h: (d, 1 - h))

    def swap_bit(self, array, which):
        return self.permute(array, lambda d, h: (d ^ (1 << which), h))

    def scatter_heads(self, blocks):
        got = self.swap_head(take(blocks, 1 - self.head, 1))
        return (take(blocks, self.head, 1).astype(f32) + got.astype(f32)).astype(bf16)

    def scatter_dp(self, blocks):
        tail = blocks.shape[1:]
        b0, b1 = self.bit(0), self.bit(1)
        first = self.head == 0
        blocks = blocks.reshape((self.n_dp // 4, 4) + tail)

        def two(one, other):
            i = jnp.where(first, one, 2 * other)
            j = jnp.where(first, 2 + one, 2 * other + 1)
            return jnp.stack([take(blocks, i, 1), take(blocks, j, 1)], axis=1)

        got = self.permute(two(1 - b0, 1 - b1), lambda d, h: (d ^ (1 if h == 0 else 2), h))
        blocks = (two(b0, b1).astype(f32) + got.astype(f32)).astype(bf16)
        mine = jnp.where(first, b1, b0)
        got = self.permute(take(blocks, 1 - mine, 1), lambda d, h: (d ^ (2 if h == 0 else 1), h))
        blocks = take(blocks, mine, 1).astype(f32) + got.astype(f32)
        for which in range(2, self.bits):
            blocks = blocks.reshape((-1, 2) + tail)
            mine = self.bit(which)
            got = self.swap_bit(take(blocks, 1 - mine, 1).astype(bf16), which)
            blocks = take(blocks, mine, 1) + got.astype(f32)
        return blocks.reshape(tail)

    def total(self, array):
        array = array + self.swap_head(array)
        for which in range(self.bits):
            array = array + self.swap_bit(array, which)
        return array


def shards(
    n_dp,
    tokens,
    lengths,
    w_qkv,
    bias_qv,
    w_out,
    bias_out,
    ln1_gain,
    ln1_bias,
    w_in,
    bias_in,
    w_down,
    bias_down,
    ln2_gain,
    ln2_bias,
    term_w,
    term_bias,
    grad_hidden,
    grad_term,
):
    links = Links(n_dp)
    head = links.head
    half, model_dim = tokens.shape
    row_len = 2 * half
    local_dim = w_qkv.shape[2]
    ffn_dim = w_in.shape[1]
    query_scale = HEAD_DIM ** (-0.5)

    boundary = jnp.cumsum(lengths[0])
    places = jnp.arange(row_len, dtype=jnp.int32)
    segment = jnp.sum((places[:, None] >= boundary[None, :]).astype(jnp.int32), axis=-1)
    seg_col = jnp.broadcast_to(segment[:, None], (row_len, LANES))
    seg_row = jnp.broadcast_to(segment[None, :], (8, row_len))

    def both(mine, theirs, axis):
        return jnp.where(
            head == 0,
            jnp.concatenate([mine, theirs], axis=axis),
            jnp.concatenate([theirs, mine], axis=axis),
        )

    group_rows = both(tokens, links.swap_head(tokens), 0)
    w_flat = w_qkv.reshape(model_dim, 3 * local_dim)
    projected = jnp.dot(group_rows, w_flat, preferred_element_type=f32)
    queries = ((projected[:, :local_dim] + bias_qv[:, 0]) * query_scale).astype(bf16)
    key_rows = projected[:, local_dim : 2 * local_dim].astype(bf16)
    value_rows = (projected[:, 2 * local_dim :] + bias_qv[:, 1]).astype(bf16)
    attended, logs = attend(lengths, queries, key_rows, value_rows, seg_col, seg_row)

    def my_half(rows):
        return lax.dynamic_slice_in_dim(rows, head * half, half, 0)

    def their_half(rows):
        return lax.dynamic_slice_in_dim(rows, (1 - head) * half, half, 0)

    token_mixed = both(my_half(attended), links.swap_head(their_half(attended)), 1)

    inputs = tokens.astype(f32)
    branch = jnp.dot(token_mixed, w_out, preferred_element_type=f32) + bias_out
    normed_one, norm_one_back = jax.vjp(layer_norm, inputs + branch, ln1_gain, ln1_bias)
    normed_low = normed_one.astype(bf16)
    hidden_pre = jnp.dot(normed_low, w_in, preferred_element_type=f32) + bias_in
    activated, gelu_back = jax.vjp(partial(jax.nn.gelu, approximate=False), hidden_pre)
    active_low = activated.astype(bf16)
    ffn_out = jnp.dot(active_low, w_down, preferred_element_type=f32) + bias_down
    normed_two, norm_two_back = jax.vjp(layer_norm, normed_one + ffn_out, ln2_gain, ln2_bias)
    term_logit = jnp.dot(normed_two, term_w, precision=highest) + term_bias[0]
    term_weight = jax.nn.softplus(term_logit)
    logit_grad = grad_term * jax.nn.sigmoid(term_logit)
    two_grad = grad_hidden + logit_grad[:, None] * term_w[None, :]
    term_w_local = jnp.dot(logit_grad, normed_two, precision=highest)
    term_bias_local = jnp.sum(logit_grad)
    resid_two_grad, gain_two_grad, shift_two_grad = norm_two_back(two_grad)
    ffn_grad = resid_two_grad.astype(bf16)
    down_local = lax.dot_general(active_low, ffn_grad, TN, preferred_element_type=f32).astype(bf16)
    bias_down_local = jnp.sum(ffn_grad.astype(f32), axis=0)
    active_grad = lax.dot_general(ffn_grad, w_down, NT, preferred_element_type=f32)
    (pre_grad,) = gelu_back(active_grad)
    pre_low = pre_grad.astype(bf16)
    in_local = lax.dot_general(normed_low, pre_low, TN, preferred_element_type=f32).astype(bf16)
    bias_in_local = jnp.sum(pre_low.astype(f32), axis=0)
    one_grad = resid_two_grad + lax.dot_general(pre_low, w_in, NT, preferred_element_type=f32)
    resid_one_grad, gain_one_grad, shift_one_grad = norm_one_back(one_grad)
    branch_low = resid_one_grad.astype(bf16)
    out_local = lax.dot_general(token_mixed, branch_low, TN, preferred_element_type=f32).astype(bf16)
    bias_out_local = jnp.sum(branch_low.astype(f32), axis=0)
    mixed_grad = lax.dot_general(branch_low, w_out, NT, preferred_element_type=f32).astype(bf16)

    my_cols = lax.dynamic_slice_in_dim(mixed_grad, head * local_dim, local_dim, 1)
    their_cols = lax.dynamic_slice_in_dim(mixed_grad, (1 - head) * local_dim, local_dim, 1)
    head_grad = both(my_cols, links.swap_head(their_cols), 0)

    raw_grad, raw_sums = attend_back(lengths, queries, key_rows, value_rows, head_grad, logs, seg_col, seg_row)

    def blocks_of(partial_sum):
        rows, cols = partial_sum.shape
        return partial_sum.reshape(n_dp, 2, rows // (2 * n_dp), cols)

    grad_down = links.scatter_dp(links.scatter_heads(blocks_of(down_local)))
    grad_in = links.scatter_dp(links.scatter_heads(blocks_of(in_local)))
    grad_out = links.scatter_dp(links.scatter_heads(blocks_of(out_local)))

    input_grad = lax.dot_general(raw_grad, w_flat, NT, preferred_element_type=f32)
    received = links.swap_head(their_half(input_grad).astype(bf16))
    grad_tokens = resid_one_grad + my_half(input_grad) + received.astype(f32)
    qkv_local = lax.dot_general(group_rows, raw_grad, TN, preferred_element_type=f32).astype(bf16)
    grad_qkv = links.scatter_dp(qkv_local.reshape(n_dp, model_dim // n_dp, 3 * local_dim))
    grad_qkv = grad_qkv.reshape(model_dim // n_dp, 3, local_dim)

    vectors = jnp.stack(
        [
            bias_out_local,
            gain_one_grad,
            shift_one_grad,
            bias_down_local,
            gain_two_grad,
            shift_two_grad,
            term_w_local,
            jnp.full((model_dim,), term_bias_local),
        ]
    )
    vectors = jnp.concatenate([vectors, bias_in_local.reshape(-1, model_dim)])
    vectors = links.total(vectors)
    place = 2 * links.dp + head
    width = model_dim // (2 * n_dp)
    mine = lax.dynamic_slice_in_dim(vectors[:8], place * width, width, 1)
    in_width = ffn_dim // (2 * n_dp)
    bias_in_mine = lax.dynamic_slice_in_dim(vectors[8:].reshape(-1), place * in_width, in_width, 0)

    padded = lax.dynamic_update_slice(
        jnp.zeros((2, 2 * local_dim), f32),
        jnp.concatenate([raw_sums[:, :local_dim], raw_sums[:, 2 * local_dim :]]),
        (jnp.int32(0), head * local_dim),
    )
    bias_qv_mine = lax.dynamic_slice_in_dim(links.total(padded), place * width, width, 1).T

    return (
        normed_two.astype(bf16),
        term_weight,
        grad_tokens,
        grad_qkv,
        bias_qv_mine,
        grad_out,
        mine[0],
        mine[1],
        mine[2],
        grad_in,
        bias_in_mine,
        grad_down,
        mine[3],
        mine[4],
        mine[5],
        mine[6],
        vectors[7, :1],
    )


def solution(mesh):
    rows = P(AXES, None)
    return jax.shard_map(
        partial(shards, mesh.shape["dp"]),
        mesh=mesh,
        in_specs=(rows, P("dp", None), P(None, None, "head"), P("head", None))
        + (P(),) * 12
        + (rows, P(AXES)),
        out_specs=(
            rows,
            P(AXES),
            rows,
            P("dp", None, "head"),
            rows,
            rows,
            P(AXES),
            P(AXES),
            P(AXES),
            rows,
            P(AXES),
            rows,
            P(AXES),
            P(AXES),
            P(AXES),
            P(AXES),
            P(),
        ),
        check_vma=False,
    )
```

time: 1300 us -> 373 us (0.29)
  waiting for transfers between devices: 491 us -> 41.6 us
  matrix products: 485 us -> 124 us
  other arithmetic: 165 us -> 37.7 us
  Pallas kernels: 0 us -> 76.8 us
  blocking collectives: 52.6 us -> 0 us
  starting transfers between devices: 0.24 us -> 38.9 us
  local copies, waits for them, and re-layouts: 82.5 us -> 46.2 us
  between operations: 16.4 us -> 2.6 us
    reduce_scatter x4 -> x0, waiting for transfers between devices: 392 us -> none  [the longest x1 142 us: shards(): lax.psum_scatter(down_local, ('dp', 'head'), scatter_dimension=0, tiled=T...]
    dot_general x40 -> x12, matrix products: 478 us -> 118 us  [the longest x1 37.4 us: shards(): hidden_pre = jnp.dot(normed_low, w_in, preferred_element_type=f32) + bias_in]
    unnamed x7 -> x0, waiting for transfers between devices: 90.8 us -> none
    convert_element_type x7 -> x8, other arithmetic: 92.4 us -> 11.9 us  [the longest x3 6.58 us: scatter_heads(): (take(blocks, self.head, 1).astype(f32) + got.astype(f32)).astype(bf16)]
    pallas_call x0 -> x2, Pallas kernels: none -> 76.8 us  [the longest x1 45.7 us: attend_back(): pl.pallas_call(attend_back_kernel, grid_spec=pltpu.PrefetchScalarGridSpec...]
    reduce_sum x9 -> x3, other arithmetic: 52.4 us -> 1.85 us  [the longest x1 1.4 us: shards(): bias_out_local = jnp.sum(branch_low.astype(f32), axis=0)]
    unnamed x1 -> x0, blocking collectives: 42.4 us -> none
    ppermute x0 -> x33, waiting for transfers between devices: none -> 41.6 us  [permute(): return lax.ppermute(array, AXES, pairs)]
  transfers between devices with their start and end apart: 6 -> 33, of which waited for: 6 -> 13; matrix products, arithmetic and copies ran while one was open for 5% -> 21% of each run, Pallas kernels for 0% -> 12%
where the time goes in v1:
time: 373 us; the launch traced here: 368 us
  matrix products  124 us (33%)
  Pallas kernels  76.8 us (21%)
  local copies, waits for them, and re-layouts  46.2 us (12%)
  waiting for transfers between devices  41.6 us (11%)
  starting transfers between devices  38.9 us (10%)
  other arithmetic  37.7 us (10%)
    pallas_call x1, Pallas kernels, attend_back(): pl.pallas_call(attend_back_kernel, grid_spec=pltpu.PrefetchScalarGridSpec...  45.7 us
    ppermute x33, waiting for transfers between devices, permute(): return lax.ppermute(array, AXES, pairs)  41.6 us
    ppermute x33, starting transfers between devices, permute(): return lax.ppermute(array, AXES, pairs)  38.9 us
    dot_general x1, matrix products, shards(): hidden_pre = jnp.dot(normed_low, w_in, preferred_element_type=f32) + bias_in  37.4 us
    pallas_call x1, Pallas kernels, attend(): pl.pallas_call(attend_kernel, grid_spec=pltpu.PrefetchScalarGridSpec(num_...  31 us
    unnamed x118, local copies, waits for them, and re-layouts  19.9 us
    dot_general x1, matrix products, shards(): lax.dot_general(ffn_grad, w_down, NT, preferred_element_type=f32)  18.5 us
    dot_general x1, matrix products, shards(): lax.dot_general(pre_low, w_in, NT, preferred_element_type=f32)  12.7 us
  transfers between devices with their start and end apart: 33, of which 13 were waited for; matrix products, arithmetic and copies ran while one was open for 21% of the time, Pallas kernels for 12%

profile of v1, /device:TPU:0, one launch (start us, length us, event | category | flops | bytes accessed | tf_op | source)
XLA Modules:
  0.0 367.9 jit_solution(10826026878390646433)
XLA Ops:
  2.1 2.6 copy.71
  4.9 7.7 %fusion.25 = f32[2048,1152]{1,0:T(8,128)S(1)} fusion(bf16[768,1152]{0,1:T(8,128)(2,1)S(1)} %bitcast.145, bf16[1024,768]{1,0:T(8,128)(2,1)} %collective-permute-done, bf16[1024,768]{1,0:T(8,128)(2,1)} %param.18, pred[]{:T(512)S(6)} %eq.2), kind=kOutput, calls=%fused_computation.90 | convolution fusion | flops 3638034432 | bytes 14352385 | tf_op jit(solution)/shard_map/dot_general | solution.py:328
  12.8 1.8 fusion.8
  15.0 31.0 %shard_map.305 = (bf16[2048,384]{1,0:T(8,128)(2,1)S(1)}, f32[8,2048]{1,0:T(8,128)S(1)}) custom-call(s32[1,32]{1,0:T(1,128)S(1)} %copy-done.5, bf16[2048,384]{1,0:T(8,128)(2,1)S(1)} %get-tuple-element.114.q_ref, bf16[2048,384]{1,0:T(8,128)(2,1)S(1)} %slice.93.k_ref, bf16[2048,384]{1,0:T(8,128)(2,1)} %get-tuple-element.113.v_ref, ...), custom_call_target="tpu_custom_call" | custom-call | flops 20000000000 | bytes 8000000 | tf_op jit(solution)/shard_map/pallas_call | solution.py:101
  50.1 3.7 copy.73
  53.8 3.2 fusion.47
  57.9 37.4 %multiply_convert_fusion = (bf16[1024,3072]{1,0:T(8,128)(2,1)S(1)}, f32[1024,3072]{1,0:T(8,128)}, f32[1024,3072]{1,0:T(8,128)}) fusion(f32[3072]{0:T(1024)S(1)} %copy-done.39, bf16[768,3072]{1,0:T(8,128)(2,1)S(1)} %bitcast.157, f32[1024,768]{0,1:T(8,128)S(1)} %get-tuple-element.147, f32[768]{0:T(1024)S(1)} %copy-done.42, f32[768]{0:T(1024)S(1)} %copy-done.35, ...), kind=kOutput, calls=%fused_computation.4 | convolution fusion | flops 5043388416 | bytes 39348224 | tf_op jit(solution)/shard_map/dot_general | solution.py:346
  95.3 6.0 %fusion.48 = (f32[1024]{0:T(1024)S(1)}, f32[1024,768]{0,1:T(8,128)S(1)}) fusion(f32[768]{0:T(1024)S(1)} %copy-done.41, bf16[1024,3072]{1,0:T(8,128)(2,1)S(1)} %get-tuple-element.111, bf16[3072,768]{1,0:T(8,128)(2,1)S(1)} %bitcast.155, f32[768]{0:T(1024)S(1)} %copy-done.42, f32[768]{0:T(1024)S(1)} %copy-done.35, f32[1024]{0:T(1024)S(1)} %fusion.30, ...), kind=kOutput, calls=%fused_computation.174 | convolution fusion | flops 4837342208 | bytes 17323008 | tf_op jit(solution)/shard_map/dot_general | solution.py:349
  102.0 2.2 fusion.14
  110.6 7.1 %convolution_convert_fusion = bf16[3072,768]{1,0:T(8,128)(2,1)} fusion(bf16[1024,3072]{1,0:T(8,128)(2,1)S(1)} %get-tuple-element.111, bf16[1024,768]{0,1:T(8,128)(2,1)S(1)} %get-tuple-element.104), kind=kOutput, calls=%fused_computation.18 | convolution fusion | flops 4834197504 | bytes 12582912 | tf_op jit(solution)/shard_map/dot_general | solution.py:359
  117.7 18.5 %convert_reduce_fusion = (f32[3072]{0:T(1024)S(1)}, bf16[1024,3072]{1,0:T(8,128)(2,1)}) fusion(f32[1024,3072]{1,0:T(8,128)} %get-tuple-element.112, bf16[1024,768]{0,1:T(8,128)(2,1)} %copy-done.22, bf16[3072,768]{1,0:T(8,128)(2,1)} %param.28, f32[1024,3072]{1,0:T(8,128)} %get-tuple-element.148, f32[3072]{0:T(1024)S(1)} %copy-done.39), kind=kOutput, calls=%fused_computation.2 | convolution fusion | flops 4885312512 | bytes 37773312 | tf_op jit(solution)/shard_map/dot_general | solution.py:361
  136.2 12.7 %multiply_reduce_fusion.1 = (f32[768]{0:T(1024)S(1)}, f32[1024]{0:T(1024)S(1)}, f32[768]{0:T(1024)}, f32[1024,768]{0,1:T(8,128)}) fusion(f32[1024,768]{0,1:T(8,128)} %copy-done.10, f32[1024]{0:T(1024)S(1)} %fusion.30, f32[1024]{0:T(1024)S(1)} %broadcast_multiply_fusion.1, f32[768]{0:T(1024)S(1)} %copy-done.35, bf16[1024,3072]{1,0:T(8,128)(2,1)} %get-tuple-element.153, ...), kind=kOutput, calls=%fused_computation.36 | convolution fusion | flops 4839699456 | bytes 20472832 | tf_op jit(solution)/shard_map/dot_general | solution.py:366
  148.9 7.5 %convolution_convert_fusion.1 = bf16[768,3072]{1,0:T(8,128)(2,1)} fusion(bf16[1024,3072]{1,0:T(8,128)(2,1)S(1)} %copy-done.43, f32[1024,768]{0,1:T(8,128)S(1)} %copy-done.11, f32[768]{0:T(1024)S(1)} %copy-done.42, f32[768]{0:T(1024)S(1)} %copy-done.35, f32[1024]{0:T(1024)S(1)} %fusion.30, f32[1024]{0:T(1024)S(1)} %broadcast_multiply_fusion.1), kind=kOutput, calls=%fused_computation.19 | convolution fusion | flops 4838129664 | bytes 14170112 | tf_op jit(solution)/shard_map/dot_general | solution.py:364
  156.4 3.5 fusion.13
  162.4 3.7 fusion.43
  170.9 2.0 concatenate.31
  173.0 3.4 convolution_convert_fusion.4
  176.5 2.6 convolution_convert_fusion.3
  179.1 3.4 collective-permute-start.19
  185.0 2.1 collective-permute-start.20
  187.1 2.7 constant_dynamic-slice_fusion.17
  189.8 2.8 collective-permute-start.21
  192.6 3.2 dynamic-slice_bitcast_fusion.1
  195.8 2.3 collective-permute-start.22
  206.3 2.9 maximum_select_fusion.2.g_ref
  209.2 45.7 %shard_map.306 = (bf16[2048,1152]{1,0:T(8,128)(2,1)}, f32[1,1152]{1,0:T(1,128)}) custom-call(s32[1,32]{1,0:T(1,128)} %lengths_ref.3, bf16[2048,384]{1,0:T(8,128)(2,1)} %copy-done.2, bf16[2048,384]{1,0:T(8,128)(2,1)} %copy-done.1, bf16[2048,384]{1,0:T(8,128)(2,1)} %get-tuple-element.113.v_ref, bf16[2048,384]{1,0:T(8,128)(2,1)} %maximum_select_fusion.2.g_ref, ...), custom_call_target="tpu_custom_call" | custom-call | flops 40000000000 | bytes 12000000 | tf_op jit(solution)/shard_map/pallas_call | solution.py:189
  255.8 7.6 %convolution_convert_fusion.2 = bf16[768,1152]{1,0:T(8,128)(2,1)S(1)} fusion(bf16[2048,1152]{1,0:T(8,128)(2,1)} %get-tuple-element.23, bf16[1024,768]{1,0:T(8,128)(2,1)} %collective-permute-done, bf16[1024,768]{1,0:T(8,128)(2,1)S(1)} %copy-done.19, pred[]{:T(512)S(6)} %eq.2), kind=kOutput, calls=%fused_computation.26 | convolution fusion | flops 3638919168 | bytes 9633793 | tf_op jit(solution)/shard_map/dot_general | solution.py:390
  264.0 1.9 collective-permute-start.4
  267.3 2.5 collective-permute-start.10
  270.0 4.5 %fusion.49 = f32[2048,768]{0,1:T(8,128)S(1)} fusion(bf16[2048,1152]{1,0:T(8,128)(2,1)S(1)} %copy-done.44, bf16[768,1152]{0,1:T(8,128)(2,1)S(1)} %bitcast.146), kind=kOutput, calls=%fused_computation.175 | convolution fusion | flops 3623878656 | bytes 12779520 | tf_op jit(solution)/shard_map/dot_general | solution.py:387
  278.2 3.2 collective-permute-start.3
  281.4 2.4 collective-permute-start.12
  284.1 1.9 collective-permute-start.5
  286.0 2.3 collective-permute-start.17
  288.9 2.0 collective-permute-done.17
  292.6 1.8 collective-permute-start.6
  294.4 2.4 fusion.6
  299.9 2.8 fusion.7
  306.3 1.9 collective-permute-start.7
  308.1 2.6 convert_add_fusion.2
  310.7 3.5 copy.85
  319.1 14.6 %collective-permute-done.24 = bf16[4,2,24,3072]{3,2,1,0:T(8,128)(2,1)} collective-permute-done((bf16[4,2,24,3072]{3,2,1,0:T(8,128)(2,1)}, bf16[4,2,24,3072]{3,2,1,0:T(8,128)(2,1)}, u32[]{:S(2)}, u32[]{:S(2)}) %collective-permute-start.24) | collective-permute-done | bytes 1179680 | tf_op jit(solution)/shard_map/ppermute | solution.py:242
  338.8 1.7 reshape_reshape.7
  344.7 1.7 collective-permute-done.25
  348.0 6.3 %collective-permute-done.31 = bf16[2,96,768]{2,1,0:T(8,128)(2,1)S(1)} collective-permute-done((bf16[2,96,768]{2,1,0:T(8,128)(2,1)S(1)}, bf16[2,96,768]{2,1,0:T(8,128)(2,1)S(1)}, u32[]{:S(2)}, u32[]{:S(2)}) %collective-permute-start.31) | collective-permute-done | bytes 294944 | tf_op jit(solution)/shard_map/ppermute | solution.py:242
  354.5 3.8 %collective-permute-done.26 = bf16[2,24,3072]{2,1,0:T(8,128)(2,1)S(1)} collective-permute-done((bf16[2,24,3072]{2,1,0:T(8,128)(2,1)S(1)}, bf16[2,24,3072]{2,1,0:T(8,128)(2,1)S(1)}, u32[]{:S(2)}, u32[]{:S(2)}) %collective-permute-start.26) | collective-permute-done | bytes 294944 | tf_op jit(solution)/shard_map/ppermute | solution.py:242
  358.5 5.2 %collective-permute-done.32 = bf16[1,96,768]{2,1,0:T(8,128)(2,1)S(1)} collective-permute-done((bf16[1,96,768]{2,1,0:T(8,128)(2,1)S(1)}, bf16[1,96,768]{2,1,0:T(8,128)(2,1)S(1)}, u32[]{:S(2)}, u32[]{:S(2)}) %collective-permute-start.32) | collective-permute-done | bytes 147488 | tf_op jit(solution)/shard_map/ppermute | solution.py:242
  364.5 2.4 collective-permute-done.27
  (258 shorter events, 64.5 us)
Async XLA Ops:
  0.7 53.1 %copy-start = (bf16[768,768]{1,0:T(8,128)(2,1)S(1)}, bf16[768,768]{1,0:T(8,128)(2,1)}, u32[]{:S(2)}) copy-start(bf16[768,768]{1,0:T(8,128)(2,1)} %param.22) | copy-start | bytes 3538948
  0.7 4.2 %collective-permute-start = (bf16[1024,768]{1,0:T(8,128)(2,1)}, bf16[1024,768]{1,0:T(8,128)(2,1)}, u32[]{:S(2)}, u32[]{:S(2)}) collective-permute-start(bf16[1024,768]{1,0:T(8,128)(2,1)} %param.18), channel_id=1, source_target_pairs={{0,1},{1,0},{2,3},{3,2},{4,5},{5,4},{6,7},{7,6},{8,9},{9,8},{10,11... | collective-permute-start | bytes 4718600 | tf_op jit(solution)/shard_map/ppermute | solution.py:242
  14.6 31.4 %copy-start.2 = (bf16[2048,384]{1,0:T(8,128)(2,1)}, bf16[2048,384]{1,0:T(8,128)(2,1)S(1)}, u32[]{:S(2)}) copy-start(bf16[2048,384]{1,0:T(8,128)(2,1)S(1)} %get-tuple-element.114.q_ref) | copy-start | bytes 4718596
  14.6 31.4 %copy-start.4 = (s32[8,2048]{1,0:T(8,128)}, s32[8,2048]{1,0:T(8,128)S(1)}, u32[]{:S(2)}) copy-start(s32[8,2048]{1,0:T(8,128)S(1)} %broadcast_in_dim.15.segr_ref) | copy-start | bytes 196612
  14.9 31.1 %copy-start.3 = (s32[2048,128]{1,0:T(8,128)}, s32[2048,128]{1,0:T(8,128)S(1)}, u32[]{:S(2)}) copy-start(s32[2048,128]{1,0:T(8,128)S(1)} %broadcast_in_dim.14.segc_ref) | copy-start | bytes 3145732
  47.2 6.6 %collective-permute-start.1 = (bf16[1024,384]{1,0:T(8,128)(2,1)}, bf16[1024,384]{1,0:T(8,128)(2,1)}, u32[]{:S(2)}, u32[]{:S(2)}) collective-permute-start(bf16[1024,384]{1,0:T(8,128)(2,1)} %get-tuple-element.131), channel_id=1, source_target_pairs={{0,1},{1,0},{2,3},{3,2},{4,5},{5,4},{6,7},{7,6},{8,9},{9,8},{10,11... | collective-permute-start | bytes 2359304 | tf_op jit(solution)/shard_map/ppermute | solution.py:242
  53.8 41.5 %slice-start.6 = ((s8[4718592]{0:T(1024)(128)(4,1)}), s8[524288]{0:T(1024)(128)(4,1)S(1)}, s32[]{:S(2)}) async-start(s8[4718592]{0:T(1024)(128)(4,1)} %bitcast.154), calls=%async_computation.6 | async-start | bytes 1048576
  57.0 38.3 %copy-start.10 = (f32[1024,768]{0,1:T(8,128)}, f32[1024,768]{0,1:T(8,128)S(1)}, u32[]{:S(2)}) copy-start(f32[1024,768]{0,1:T(8,128)S(1)} %get-tuple-element.147) | copy-start | bytes 9437188
  57.5 37.8 %copy-start.33 = (f32[1024]{0:T(1024)}, f32[1024]{0:T(1024)S(1)}, u32[]{:S(2)}) copy-start(f32[1024]{0:T(1024)S(1)} %multiply_reduce_fusion.5) | copy-start | bytes 12292
  57.8 37.5 %slice-start.7 = ((s8[4718592]{0:T(1024)(128)(4,1)}), s8[4194304]{0:T(1024)(128)(4,1)S(1)}, s32[]{:S(2)}) async-start(s8[4718592]{0:T(1024)(128)(4,1)} %bitcast.154), calls=%async_computation.7 | async-start | bytes 8388608
  57.9 37.5 %copy-start.41 = (f32[768]{0:T(1024)S(1)}, f32[768]{0:T(1024)}, u32[]{:S(2)}) copy-start(f32[768]{0:T(1024)} %param.29) | copy-start | bytes 9220
  172.9 6.2 %collective-permute-start.18 = (f32[12,768]{1,0:T(8,128)}, f32[12,768]{1,0:T(8,128)S(1)}, u32[]{:S(2)}, u32[]{:S(2)}) collective-permute-start(f32[12,768]{1,0:T(8,128)} %concatenate.31), channel_id=1, source_target_pairs={{0,1},{1,0},{2,3},{3,2},{4,5},{5,4},{6,7},{7,6},{8,9},{9,8},{10,11... | collective-permute-start | bytes 110600 | tf_op jit(solution)/shard_map/ppermute | solution.py:242
  179.1 5.8 %collective-permute-start.19 = (f32[12,768]{1,0:T(8,128)S(1)}, f32[12,768]{1,0:T(8,128)S(1)}, u32[]{:S(2)}, u32[]{:S(2)}) collective-permute-start(f32[12,768]{1,0:T(8,128)S(1)} %add.406), channel_id=1, source_target_pairs={{0,2},{1,3},{2,0},{3,1},{4,6},{5,7},{6,4},{7,5},{8,10},{9,11},{10,... | collective-permute-start | bytes 110600 | tf_op jit(solution)/shard_map/ppermute | solution.py:242
  185.0 18.2 %collective-permute-start.13 = (bf16[16,24,768]{2,1,0:T(8,128)(2,1)}, bf16[16,24,768]{2,1,0:T(8,128)(2,1)}, u32[]{:S(2)}, u32[]{:S(2)}) collective-permute-start(bf16[16,24,768]{2,1,0:T(8,128)(2,1)} %dynamic-slice_bitcast_fusion.4), channel_id=1, source_target_pairs={{0,1},{1,0},{2,3},{3,2},{4,5},{5,4},{6,7},{7,6},{8,9},{9,8},{10,11... | collective-permute-start | bytes 1769480 | tf_op jit(solution)/shard_map/ppermute | solution.py:242
  185.0 4.8 %collective-permute-start.20 = (f32[12,768]{1,0:T(8,128)S(1)}, f32[12,768]{1,0:T(8,128)S(1)}, u32[]{:S(2)}, u32[]{:S(2)}) collective-permute-start(f32[12,768]{1,0:T(8,128)S(1)} %add.407), channel_id=1, source_target_pairs={{0,4},{1,5},{2,6},{3,7},{4,0},{5,1},{6,2},{7,3},{8,12},{9,13},{10,... | collective-permute-start | bytes 110600 | tf_op jit(solution)/shard_map/ppermute | solution.py:242
  189.8 16.4 %collective-permute-start.2 = (bf16[1024,384]{1,0:T(8,128)(2,1)}, bf16[1024,384]{1,0:T(8,128)(2,1)}, u32[]{:S(2)}, u32[]{:S(2)}) collective-permute-start(bf16[1024,384]{1,0:T(8,128)(2,1)} %get-tuple-element.129), channel_id=1, source_target_pairs={{0,1},{1,0},{2,3},{3,2},{4,5},{5,4},{6,7},{7,6},{8,9},{9,8},{10,11... | collective-permute-start | bytes 2359304 | tf_op jit(solution)/shard_map/ppermute | solution.py:242
  189.8 6.0 %collective-permute-start.21 = (f32[12,768]{1,0:T(8,128)S(1)}, f32[12,768]{1,0:T(8,128)S(1)}, u32[]{:S(2)}, u32[]{:S(2)}) collective-permute-start(f32[12,768]{1,0:T(8,128)S(1)} %add.408), channel_id=1, source_target_pairs={{0,8},{1,9},{2,10},{3,11},{4,12},{5,13},{6,14},{7,15},{8,0},{9,1},... | collective-permute-start | bytes 110600 | tf_op jit(solution)/shard_map/ppermute | solution.py:242
  195.8 5.6 %collective-permute-start.22 = (f32[12,768]{1,0:T(8,128)S(1)}, f32[12,768]{1,0:T(8,128)S(1)}, u32[]{:S(2)}, u32[]{:S(2)}) collective-permute-start(f32[12,768]{1,0:T(8,128)S(1)} %add.409), channel_id=1, source_target_pairs={{0,16},{1,17},{2,18},{3,19},{4,20},{5,21},{6,22},{7,23},{8,24},{9,... | collective-permute-start | bytes 110600 | tf_op jit(solution)/shard_map/ppermute | solution.py:242
  199.8 94.6 %collective-permute-start.28 = (bf16[16,96,768]{2,1,0:T(8,128)(2,1)}, bf16[16,96,768]{2,1,0:T(8,128)(2,1)}, u32[]{:S(2)}, u32[]{:S(2)}) collective-permute-start(bf16[16,96,768]{2,1,0:T(8,128)(2,1)} %dynamic-slice_bitcast_fusion), channel_id=1, source_target_pairs={{0,1},{1,0},{2,3},{3,2},{4,5},{5,4},{6,7},{7,6},{8,9},{9,8},{10,11... | collective-permute-start | bytes 7077896 | tf_op jit(solution)/shard_map/ppermute | solution.py:242
  199.8 100.1 %collective-permute-start.23 = (bf16[16,24,3072]{2,1,0:T(8,128)(2,1)}, bf16[16,24,3072]{2,1,0:T(8,128)(2,1)}, u32[]{:S(2)}, u32[]{:S(2)}) collective-permute-start(bf16[16,24,3072]{2,1,0:T(8,128)(2,1)} %dynamic-slice_bitcast_fusion.1), channel_id=1, source_target_pairs={{0,1},{1,0},{2,3},{3,2},{4,5},{5,4},{6,7},{7,6},{8,9},{9,8},{10,11... | collective-permute-start | bytes 7077896 | tf_op jit(solution)/shard_map/ppermute | solution.py:242
  204.7 65.1 %collective-permute-start.14 = (bf16[4,2,24,768]{3,2,1,0:T(8,128)(2,1)S(1)}, bf16[4,2,24,768]{3,2,1,0:T(8,128)(2,1)S(1)}, u32[]{:S(2)}, u32[]{:S(2)}) collective-permute-start(bf16[4,2,24,768]{3,2,1,0:T(8,128)(2,1)S(1)} %pad_maximum_fusion.3), channel_id=1, source_target_pairs={{0,2},{1,5},{2,0},{3,7},{4,6},{5,1},{6,4},{7,3},{8,10},{9,13},{10,... | collective-permute-start | bytes 884744 | tf_op jit(solution)/shard_map/ppermute | solution.py:242
  209.2 46.5 %copy-start.19 = (bf16[1024,768]{1,0:T(8,128)(2,1)S(1)}, bf16[1024,768]{1,0:T(8,128)(2,1)}, u32[]{:S(2)}) copy-start(bf16[1024,768]{1,0:T(8,128)(2,1)} %param.18) | copy-start | bytes 4718596
  255.7 7.9 %collective-permute-start.8 = (f32[2,768]{1,0:T(2,128)S(1)}, f32[2,768]{1,0:T(2,128)S(1)}, u32[]{:S(2)}, u32[]{:S(2)}) collective-permute-start(f32[2,768]{1,0:T(2,128)S(1)} %constant_dynamic-update-slice_fusion.1), channel_id=1, source_target_pairs={{0,1},{1,0},{2,3},{3,2},{4,5},{5,4},{6,7},{7,6},{8,9},{9,8},{10,11... | collective-permute-start | bytes 18440 | tf_op jit(solution)/shard_map/ppermute | solution.py:242
  263.6 3.7 %collective-permute-start.9 = (f32[2,768]{1,0:T(2,128)S(1)}, f32[2,768]{1,0:T(2,128)S(1)}, u32[]{:S(2)}, u32[]{:S(2)}) collective-permute-start(f32[2,768]{1,0:T(2,128)S(1)} %constant_dynamic-update-slice_fusion), channel_id=1, source_target_pairs={{0,2},{1,3},{2,0},{3,1},{4,6},{5,7},{6,4},{7,5},{8,10},{9,11},{10,... | collective-permute-start | bytes 18440 | tf_op jit(solution)/shard_map/ppermute | solution.py:242
  264.0 19.8 %collective-permute-start.4 = (bf16[4,2,48,1152]{3,2,0,1:T(8,128)(2,1)S(1)}, bf16[4,2,48,1152]{3,2,0,1:T(8,128)(2,1)S(1)}, u32[]{:S(2)}, u32[]{:S(2)}) collective-permute-start(bf16[4,2,48,1152]{3,2,0,1:T(8,128)(2,1)S(1)} %pad_maximum_fusion.2), channel_id=1, source_target_pairs={{0,2},{1,5},{2,0},{3,7},{4,6},{5,1},{6,4},{7,3},{8,10},{9,13},{10,... | collective-permute-start | bytes 2654216 | tf_op jit(solution)/shard_map/ppermute | solution.py:242
  267.3 7.2 %collective-permute-start.10 = (f32[2,768]{1,0:T(2,128)S(1)}, f32[2,768]{1,0:T(2,128)S(1)}, u32[]{:S(2)}, u32[]{:S(2)}) collective-permute-start(f32[2,768]{1,0:T(2,128)S(1)} %add.393), channel_id=1, source_target_pairs={{0,4},{1,5},{2,6},{3,7},{4,0},{5,1},{6,2},{7,3},{8,12},{9,13},{10,... | collective-permute-start | bytes 18440 | tf_op jit(solution)/shard_map/ppermute | solution.py:242
  269.9 24.5 %slice-start.4 = ((s8[4718592]{0:T(1024)(128)(4,1)}), s8[4194304]{0:T(1024)(128)(4,1)S(1)}, s32[]{:S(2)}) async-start(s8[4718592]{0:T(1024)(128)(4,1)} %bitcast.135), calls=%async_computation.4 | async-start | bytes 8388608
  269.9 24.5 %slice-start.5 = ((s8[4718592]{0:T(1024)(128)(4,1)}), s8[524288]{0:T(1024)(128)(4,1)S(1)}, s32[]{:S(2)}) async-start(s8[4718592]{0:T(1024)(128)(4,1)} %bitcast.135), calls=%async_computation.5 | async-start | bytes 1048576
  269.9 6.8 %collective-permute-start.15 = (bf16[4,24,768]{2,1,0:T(8,128)(2,1)S(1)}, bf16[4,24,768]{2,1,0:T(8,128)(2,1)S(1)}, u32[]{:S(2)}, u32[]{:S(2)}) collective-permute-start(bf16[4,24,768]{2,1,0:T(8,128)(2,1)S(1)} %dynamic-slice_bitcast_fusion.10), channel_id=1, source_target_pairs={{0,4},{1,3},{2,6},{3,1},{4,0},{5,7},{6,2},{7,5},{8,12},{9,11},{10,... | collective-permute-start | bytes 442376 | tf_op jit(solution)/shard_map/ppermute | solution.py:242
  274.5 3.7 %collective-permute-start.11 = (f32[2,768]{1,0:T(2,128)S(1)}, f32[2,768]{1,0:T(2,128)S(1)}, u32[]{:S(2)}, u32[]{:S(2)}) collective-permute-start(f32[2,768]{1,0:T(2,128)S(1)} %add.394), channel_id=1, source_target_pairs={{0,8},{1,9},{2,10},{3,11},{4,12},{5,13},{6,14},{7,15},{8,0},{9,1},... | collective-permute-start | bytes 18440 | tf_op jit(solution)/shard_map/ppermute | solution.py:242
  276.8 4.5 %collective-permute-start.16 = (bf16[2,24,768]{2,1,0:T(8,128)(2,1)S(1)}, bf16[2,24,768]{2,1,0:T(8,128)(2,1)S(1)}, u32[]{:S(2)}, u32[]{:S(2)}) collective-permute-start(bf16[2,24,768]{2,1,0:T(8,128)(2,1)S(1)} %fusion.29), channel_id=1, source_target_pairs={{0,8},{1,9},{2,10},{3,11},{4,12},{5,13},{6,14},{7,15},{8,0},{9,1},... | collective-permute-start | bytes 221192 | tf_op jit(solution)/shard_map/ppermute | solution.py:242
  278.2 29.9 %collective-permute-start.3 = (bf16[1024,768]{0,1:T(8,128)(2,1)S(1)}, bf16[1024,768]{0,1:T(8,128)(2,1)S(1)}, u32[]{:S(2)}, u32[]{:S(2)}) collective-permute-start(bf16[1024,768]{0,1:T(8,128)(2,1)S(1)} %dynamic-slice_convert_fusion), channel_id=1, source_target_pairs={{0,1},{1,0},{2,3},{3,2},{4,5},{5,4},{6,7},{7,6},{8,9},{9,8},{10,11... | collective-permute-start | bytes 4718600 | tf_op jit(solution)/shard_map/ppermute | solution.py:242
  281.4 4.6 %collective-permute-start.12 = (f32[2,768]{1,0:T(2,128)S(1)}, f32[2,768]{1,0:T(2,128)S(1)}, u32[]{:S(2)}, u32[]{:S(2)}) collective-permute-start(f32[2,768]{1,0:T(2,128)S(1)} %add.395), channel_id=1, source_target_pairs={{0,16},{1,17},{2,18},{3,19},{4,20},{5,21},{6,22},{7,23},{8,24},{9,... | collective-permute-start | bytes 18440 | tf_op jit(solution)/shard_map/ppermute | solution.py:242
  284.1 8.4 %collective-permute-start.5 = (bf16[4,48,1152]{2,1,0:T(8,128)(2,1)S(1)}, bf16[4,48,1152]{2,1,0:T(8,128)(2,1)S(1)}, u32[]{:S(2)}, u32[]{:S(2)}) collective-permute-start(bf16[4,48,1152]{2,1,0:T(8,128)(2,1)S(1)} %dynamic-slice_bitcast_fusion.5), channel_id=1, source_target_pairs={{0,4},{1,3},{2,6},{3,1},{4,0},{5,7},{6,2},{7,5},{8,12},{9,11},{10,... | collective-permute-start | bytes 1327112 | tf_op jit(solution)/shard_map/ppermute | solution.py:242
  286.0 4.9 %collective-permute-start.17 = (bf16[1,24,768]{2,1,0:T(8,128)(2,1)S(1)}, bf16[1,24,768]{2,1,0:T(8,128)(2,1)S(1)}, u32[]{:S(2)}, u32[]{:S(2)}) collective-permute-start(bf16[1,24,768]{2,1,0:T(8,128)(2,1)S(1)} %dynamic-slice_convert_fusion.8), channel_id=1, source_target_pairs={{0,16},{1,17},{2,18},{3,19},{4,20},{5,21},{6,22},{7,23},{8,24},{9,... | collective-permute-start | bytes 110600 | tf_op jit(solution)/shard_map/ppermute | solution.py:242
  292.6 12.9 %collective-permute-start.6 = (bf16[2,48,1152]{2,1,0:T(8,128)(2,1)S(1)}, bf16[2,48,1152]{2,1,0:T(8,128)(2,1)S(1)}, u32[]{:S(2)}, u32[]{:S(2)}) collective-permute-start(bf16[2,48,1152]{2,1,0:T(8,128)(2,1)S(1)} %fusion.28), channel_id=1, source_target_pairs={{0,8},{1,9},{2,10},{3,11},{4,12},{5,13},{6,14},{7,15},{8,0},{9,1},... | collective-permute-start | bytes 663560 | tf_op jit(solution)/shard_map/ppermute | solution.py:242
  298.1 16.4 %collective-permute-start.29 = (bf16[4,2,96,768]{3,2,1,0:T(8,128)(2,1)}, bf16[4,2,96,768]{3,2,1,0:T(8,128)(2,1)S(1)}, u32[]{:S(2)}, u32[]{:S(2)}) collective-permute-start(bf16[4,2,96,768]{3,2,1,0:T(8,128)(2,1)} %pad_maximum_fusion.1), channel_id=1, source_target_pairs={{0,2},{1,5},{2,0},{3,7},{4,6},{5,1},{6,4},{7,3},{8,10},{9,13},{10,... | collective-permute-start | bytes 3538952 | tf_op jit(solution)/shard_map/ppermute | solution.py:242
  305.2 28.5 %collective-permute-start.24 = (bf16[4,2,24,3072]{3,2,1,0:T(8,128)(2,1)}, bf16[4,2,24,3072]{3,2,1,0:T(8,128)(2,1)}, u32[]{:S(2)}, u32[]{:S(2)}) collective-permute-start(bf16[4,2,24,3072]{3,2,1,0:T(8,128)(2,1)} %pad_maximum_fusion), channel_id=1, source_target_pairs={{0,2},{1,5},{2,0},{3,7},{4,6},{5,1},{6,4},{7,3},{8,10},{9,13},{10,... | collective-permute-start | bytes 3538952 | tf_op jit(solution)/shard_map/ppermute | solution.py:242
  306.3 30.9 %collective-permute-start.7 = (bf16[1,48,1152]{2,1,0:T(8,128)(2,1)}, bf16[1,48,1152]{2,1,0:T(8,128)(2,1)}, u32[]{:S(2)}, u32[]{:S(2)}) collective-permute-start(bf16[1,48,1152]{2,1,0:T(8,128)(2,1)} %dynamic-slice_convert_fusion.6), channel_id=1, source_target_pairs={{0,16},{1,17},{2,18},{3,19},{4,20},{5,21},{6,22},{7,23},{8,24},{9,... | collective-permute-start | bytes 331784 | tf_op jit(solution)/shard_map/ppermute | solution.py:242
  314.3 19.4 %copy-start.14 = (bf16[4,1,24,3072]{3,2,1,0:T(8,128)(2,1)S(1)}, bf16[4,1,24,3072]{3,2,1,0:T(8,128)(2,1)}, u32[]{:S(2)}) copy-start(bf16[4,1,24,3072]{3,2,1,0:T(8,128)(2,1)} %get-tuple-element.120) | copy-start | bytes 1769476
  314.3 19.4 %copy-start.15 = (bf16[4,1,24,3072]{3,2,1,0:T(8,128)(2,1)S(1)}, bf16[4,1,24,3072]{3,2,1,0:T(8,128)(2,1)}, u32[]{:S(2)}) copy-start(bf16[4,1,24,3072]{3,2,1,0:T(8,128)(2,1)} %get-tuple-element.123) | copy-start | bytes 1769476
  317.2 20.0 %copy-start.24 = (f32[2,48,1152]{2,1,0:T(8,128)S(1)}, f32[2,48,1152]{2,1,0:T(8,128)}, u32[]{:S(2)}) copy-start(f32[2,48,1152]{2,1,0:T(8,128)} %copy-done.23) | copy-start | bytes 1327108
  318.1 24.2 %collective-permute-start.30 = (bf16[4,96,768]{2,1,0:T(8,128)(2,1)}, bf16[4,96,768]{2,1,0:T(8,128)(2,1)}, u32[]{:S(2)}, u32[]{:S(2)}) collective-permute-start(bf16[4,96,768]{2,1,0:T(8,128)(2,1)} %dynamic-slice_bitcast_fusion.2), channel_id=1, source_target_pairs={{0,4},{1,3},{2,6},{3,1},{4,0},{5,7},{6,2},{7,5},{8,12},{9,11},{10,... | collective-permute-start | bytes 1769480 | tf_op jit(solution)/shard_map/ppermute | solution.py:242
  336.2 10.2 %collective-permute-start.25 = (bf16[4,24,3072]{2,1,0:T(8,128)(2,1)}, bf16[4,24,3072]{2,1,0:T(8,128)(2,1)}, u32[]{:S(2)}, u32[]{:S(2)}) collective-permute-start(bf16[4,24,3072]{2,1,0:T(8,128)(2,1)} %dynamic-slice_bitcast_fusion.3), channel_id=1, source_target_pairs={{0,4},{1,3},{2,6},{3,1},{4,0},{5,7},{6,2},{7,5},{8,12},{9,11},{10,... | collective-permute-start | bytes 1769480 | tf_op jit(solution)/shard_map/ppermute | solution.py:242
  343.4 10.9 %collective-permute-start.31 = (bf16[2,96,768]{2,1,0:T(8,128)(2,1)S(1)}, bf16[2,96,768]{2,1,0:T(8,128)(2,1)S(1)}, u32[]{:S(2)}, u32[]{:S(2)}) collective-permute-start(bf16[2,96,768]{2,1,0:T(8,128)(2,1)S(1)} %fusion.27), channel_id=1, source_target_pairs={{0,8},{1,9},{2,10},{3,11},{4,12},{5,13},{6,14},{7,15},{8,0},{9,1},... | collective-permute-start | bytes 884744 | tf_op jit(solution)/shard_map/ppermute | solution.py:242
  347.6 10.7 %collective-permute-start.26 = (bf16[2,24,3072]{2,1,0:T(8,128)(2,1)S(1)}, bf16[2,24,3072]{2,1,0:T(8,128)(2,1)S(1)}, u32[]{:S(2)}, u32[]{:S(2)}) collective-permute-start(bf16[2,24,3072]{2,1,0:T(8,128)(2,1)S(1)} %fusion.26), channel_id=1, source_target_pairs={{0,8},{1,9},{2,10},{3,11},{4,12},{5,13},{6,14},{7,15},{8,0},{9,1},... | collective-permute-start | bytes 884744 | tf_op jit(solution)/shard_map/ppermute | solution.py:242
  354.4 9.3 %collective-permute-start.32 = (bf16[1,96,768]{2,1,0:T(8,128)(2,1)S(1)}, bf16[1,96,768]{2,1,0:T(8,128)(2,1)S(1)}, u32[]{:S(2)}, u32[]{:S(2)}) collective-permute-start(bf16[1,96,768]{2,1,0:T(8,128)(2,1)S(1)} %dynamic-slice_convert_fusion.4), channel_id=1, source_target_pairs={{0,16},{1,17},{2,18},{3,19},{4,20},{5,21},{6,22},{7,23},{8,24},{9,... | collective-permute-start | bytes 442376 | tf_op jit(solution)/shard_map/ppermute | solution.py:242
  358.4 8.5 %collective-permute-start.27 = (bf16[1,24,3072]{2,1,0:T(8,128)(2,1)S(1)}, bf16[1,24,3072]{2,1,0:T(8,128)(2,1)S(1)}, u32[]{:S(2)}, u32[]{:S(2)}) collective-permute-start(bf16[1,24,3072]{2,1,0:T(8,128)(2,1)S(1)} %dynamic-slice_convert_fusion.5), channel_id=1, source_target_pairs={{0,16},{1,17},{2,18},{3,19},{4,20},{5,21},{6,22},{7,23},{8,24},{9,... | collective-permute-start | bytes 442376 | tf_op jit(solution)/shard_map/ppermute | solution.py:242
  (40 other events, 199.6 us)

commit v2 on v1

--- a/solution.py
+++ b/solution.py
@@ -15,16 +15,9 @@
 
 f32 = jnp.float32
 bf16 = jnp.bfloat16
-highest = lax.Precision.HIGHEST
 norm_eps = 1e-06
 NT = (((1,), (1,)), ((), ()))
 TN = (((0,), (0,)), ((), ()))
-
-
-def layer_norm(resid, gain, shift):
-    center = resid - jnp.mean(resid, axis=-1, keepdims=True)
-    spread = jnp.mean(center * center, axis=-1, keepdims=True)
-    return center * lax.rsqrt(spread + norm_eps) * gain + shift
 
 
 def key_range(lengths_ref, first, rows, row_len):
@@ -126,7 +119,7 @@
 
 
 def attend_back_kernel(
-    lengths_ref, q_ref, k_ref, v_ref, g_ref, log_ref, segc_ref, segr_ref, raw_ref, sums_ref, mask_ref, dk_ref, dv_ref
+    first_pair, lengths_ref, q_ref, k_ref, v_ref, g_ref, log_ref, segc_ref, segr_ref, raw_ref, sums_ref, mask_ref, dk_ref, dv_ref
 ):
     rows, local_dim = q_ref.shape
     row_len = k_ref.shape[0]
@@ -155,7 +148,7 @@
                 q_one = jnp.where(mine, q_pair, jnp.zeros_like(q_pair))
                 g_one = jnp.where(mine, g_pair, jnp.zeros_like(g_pair))
                 scores = lax.dot_general(k_pair, q_one, NT, preferred_element_type=f32)
-                probs = jnp.exp(scores + mask_ref[:width, :] - log_ref[pl.ds(2 * pair + h, 1), :])
+                probs = jnp.exp(scores + mask_ref[:width, :] - log_ref[pl.ds(2 * (first_pair + pair) + h, 1), :])
                 dv_one = jnp.dot(probs.astype(bf16), g_one, preferred_element_type=f32)
                 prob_grad = lax.dot_general(v_pair, g_one, NT, preferred_element_type=f32)
                 inner = jnp.sum(probs * prob_grad, axis=0, keepdims=True)
@@ -181,13 +174,15 @@
         sums_ref[...] = jnp.sum(raw_ref[...].astype(f32), axis=0, keepdims=True)
 
 
-def attend_back(lengths, queries, key_rows, value_rows, grads, logs, seg_col, seg_row):
-    row_len, local_dim = queries.shape
+def attend_back(lengths, queries, key_rows, value_rows, grads, logs, seg_col, seg_row, first_pair, pairs):
+    row_len = queries.shape[0]
+    local_dim = pairs * LANES
+    place = first_pair // pairs
     rows = min(Q_ROWS, row_len)
-    whole = pl.BlockSpec((row_len, local_dim), lambda i, n: (0, 0))
-    block = pl.BlockSpec((rows, local_dim), lambda i, n: (i, 0))
+    whole = pl.BlockSpec((row_len, local_dim), lambda i, n: (0, place))
+    block = pl.BlockSpec((rows, local_dim), lambda i, n: (i, place))
     return pl.pallas_call(
-        attend_back_kernel,
+        partial(attend_back_kernel, first_pair),
         grid_spec=pltpu.PrefetchScalarGridSpec(
             num_scalar_prefetch=1,
             grid=(row_len // rows,),
@@ -215,8 +210,650 @@
             jax.ShapeDtypeStruct((1, 3 * local_dim), f32),
         ],
         compiler_params=pltpu.CompilerParams(vmem_limit_bytes=56 * 2**20),
-        cost_estimate=pl.CostEstimate(flops=40_000_000_000, bytes_accessed=12_000_000, transcendentals=0),
+        cost_estimate=pl.CostEstimate(flops=14_000_000_000 * pairs, bytes_accessed=4_000_000 * pairs, transcendentals=0),
     )(lengths, queries, key_rows, value_rows, grads, logs, seg_col, seg_row)
+
+
+ERF_TOP = (0.00022905065861350646, 0.0034082910107109506, 0.050955695062380861, 0.18520832239976145, 1.128379143519084)
+ERF_LOW = (
+    -1.1791602954361697e-7,
+    0.000023547966471313185,
+    0.0010179625278914885,
+    0.014070470171167667,
+    0.11098505178285362,
+    0.49746925110067538,
+    1.0,
+)
+TILE = 256
+CHUNK = 384
+
+
+def polynomial(x, factors):
+    value = jnp.full_like(x, factors[0])
+    for factor in factors[1:]:
+        value = value * x + factor
+    return value
+
+
+def gelu_both(x):
+    scaled = jnp.clip(x * 0.7071067811865476, -3.832506856900711, 3.832506856900711)
+    square = scaled * scaled
+    erf = scaled * polynomial(square, ERF_TOP) / polynomial(square, ERF_LOW)
+    cdf = 0.5 + 0.5 * erf
+    density = jnp.exp(-0.5 * x * x) * 0.3989422804014327
+    return x * cdf, cdf + x * density
+
+
+def normalize(resid):
+    center = resid - jnp.mean(resid, axis=-1, keepdims=True)
+    scale = lax.rsqrt(jnp.mean(center * center, axis=-1, keepdims=True) + norm_eps)
+    return center * scale, scale
+
+
+def normalize_back(grad, normed, scale):
+    shift = jnp.mean(grad, axis=-1, keepdims=True)
+    slope = jnp.mean(grad * normed, axis=-1, keepdims=True)
+    return scale * (grad - shift - normed * slope)
+
+
+def column_sum(x):
+    return jnp.sum(x.astype(f32), axis=0, keepdims=True)
+
+
+def middle_kernel(
+    mine_ref,
+    theirs_ref,
+    tokens_ref,
+    hid_ref,
+    term_ref,
+    w_out_ref,
+    w_in_ref,
+    w_down_ref,
+    vec_ref,
+    bias_in_ref,
+    term_bias_ref,
+    hidden_ref,
+    weight_ref,
+    left_ref,
+    right_ref,
+    resid_ref,
+    my_grad_ref,
+    their_grad_ref,
+    sums_ref,
+    in_sums_ref,
+    slope_ref,
+):
+    head = lax.axis_index("head")
+    local_dim = mine_ref.shape[1]
+    ffn_dim = w_in_ref.shape[1]
+    bias_out, ln1_gain, ln1_bias = vec_ref[0:1], vec_ref[1:2], vec_ref[2:3]
+    bias_down, ln2_gain, ln2_bias, term_w = vec_ref[3:4], vec_ref[4:5], vec_ref[5:6], vec_ref[6:7]
+
+    @pl.when(pl.program_id(0) == 0)
+    def _():
+        sums_ref[...] = jnp.zeros_like(sums_ref)
+        in_sums_ref[...] = jnp.zeros_like(in_sums_ref)
+
+    model_dim = w_out_ref.shape[0]
+    parts = ffn_dim // model_dim
+    left_ref[parts + 1, :, pl.ds(pl.multiple_of(head * local_dim, LANES), local_dim)] = mine_ref[...]
+    left_ref[parts + 1, :, pl.ds(pl.multiple_of((1 - head) * local_dim, LANES), local_dim)] = theirs_ref[...]
+    branch = jnp.dot(left_ref[parts + 1], w_out_ref[...], preferred_element_type=f32) + bias_out
+    normal_one, scale_one = normalize(tokens_ref[...].astype(f32) + branch)
+    normed_one = normal_one * ln1_gain + ln1_bias
+    normed_low = normed_one.astype(bf16)
+    left_ref[parts] = normed_low
+    resid = normed_one + bias_down
+    for c in range(0, ffn_dim, CHUNK):
+        cols = slice(c, c + CHUNK)
+        pre = jnp.dot(normed_low, w_in_ref[:, cols], preferred_element_type=f32) + bias_in_ref[:, cols]
+        value, slope = gelu_both(pre)
+        value = value.astype(bf16)
+        left_ref[c // model_dim, :, c % model_dim : c % model_dim + CHUNK] = value
+        slope_ref[:, cols] = slope
+        resid = resid + jnp.dot(value, w_down_ref[cols, :], preferred_element_type=f32)
+    normal_two, scale_two = normalize(resid)
+    normed_two = normal_two * ln2_gain + ln2_bias
+    hidden_ref[...] = normed_two.astype(bf16)
+    logit = jnp.sum(normed_two * term_w, axis=-1, keepdims=True) + term_bias_ref[0:1, 0:1]
+    small = jnp.exp(-jnp.abs(logit))
+    weight_ref[...] = jnp.maximum(logit, 0.0) + jnp.log1p(small)
+    logit_grad = term_ref[...] * (jnp.where(logit >= 0.0, 1.0, small) / (1.0 + small))
+    two_grad = hid_ref[...] + logit_grad * term_w
+    resid_two = normalize_back(two_grad * ln2_gain, normal_two, scale_two)
+    ffn_grad = resid_two.astype(bf16)
+    right_ref[0] = ffn_grad
+    one_grad = resid_two
+    for c in range(0, ffn_dim, CHUNK):
+        cols = slice(c, c + CHUNK)
+        active_grad = lax.dot_general(ffn_grad, w_down_ref[cols, :], NT, preferred_element_type=f32)
+        pre = (active_grad * slope_ref[:, cols]).astype(bf16)
+        right_ref[1 + c // model_dim, :, c % model_dim : c % model_dim + CHUNK] = pre
+        in_sums_ref[:, cols] += column_sum(pre)
+        one_grad = one_grad + lax.dot_general(pre, w_in_ref[:, cols], NT, preferred_element_type=f32)
+    resid_one = normalize_back(one_grad * ln1_gain, normal_one, scale_one)
+    resid_ref[...] = resid_one
+    branch_low = resid_one.astype(bf16)
+    right_ref[parts + 1] = branch_low
+    grads = lax.dot_general(branch_low, w_out_ref[...], NT, preferred_element_type=f32).astype(bf16)
+
+    @pl.when(head == 0)
+    def _():
+        my_grad_ref[...] = grads[:, :local_dim]
+        their_grad_ref[...] = grads[:, local_dim:]
+
+    @pl.when(head == 1)
+    def _():
+        my_grad_ref[...] = grads[:, local_dim:]
+        their_grad_ref[...] = grads[:, :local_dim]
+
+    sums_ref[0:1] += column_sum(branch_low)
+    sums_ref[1:2] += column_sum(one_grad * normal_one)
+    sums_ref[2:3] += column_sum(one_grad)
+    sums_ref[3:4] += column_sum(ffn_grad)
+    sums_ref[4:5] += column_sum(two_grad * normal_two)
+    sums_ref[5:6] += column_sum(two_grad)
+    sums_ref[6:7] += column_sum(logit_grad * normed_two)
+    sums_ref[7:8] += jnp.sum(logit_grad, axis=0, keepdims=True)
+
+
+def middle(mine, theirs, tokens, grad_hidden, grad_term, w_out, w_in, w_down, vec, bias_in, term_bias):
+    half, model_dim = tokens.shape
+    local_dim = mine.shape[1]
+    ffn_dim = w_in.shape[1]
+    rows = min(TILE, half)
+
+    def tile(cols):
+        return pl.BlockSpec((rows, cols), lambda i: (i, 0))
+
+    def whole(*shape):
+        return pl.BlockSpec(shape, lambda i: (0, 0), pipeline_mode=pl.Buffered(1))
+
+    stacked = pl.BlockSpec((ffn_dim // model_dim + 2, rows, model_dim), lambda i: (0, i, 0))
+    stack = jax.ShapeDtypeStruct((ffn_dim // model_dim + 2, half, model_dim), bf16)
+
+    def full(cols, kind):
+        return jax.ShapeDtypeStruct((half, cols), kind)
+
+    return pl.pallas_call(
+        middle_kernel,
+        grid=(half // rows,),
+        in_specs=[
+            tile(local_dim),
+            tile(local_dim),
+            tile(model_dim),
+            tile(model_dim),
+            tile(1),
+            whole(model_dim, model_dim),
+            whole(model_dim, ffn_dim),
+            whole(ffn_dim, model_dim),
+            whole(8, model_dim),
+            whole(1, ffn_dim),
+            whole(1, 1),
+        ],
+        out_specs=[
+            tile(model_dim),
+            tile(1),
+            stacked,
+            stacked,
+            tile(model_dim),
+            tile(local_dim),
+            tile(local_dim),
+            pl.BlockSpec((8, model_dim), lambda i: (0, 0)),
+            pl.BlockSpec((1, ffn_dim), lambda i: (0, 0)),
+        ],
+        scratch_shapes=[pltpu.VMEM((rows, ffn_dim), f32)],
+        out_shape=[
+            full(model_dim, bf16),
+            full(1, f32),
+            stack,
+            stack,
+            full(model_dim, f32),
+            full(local_dim, bf16),
+            full(local_dim, bf16),
+            jax.ShapeDtypeStruct((8, model_dim), f32),
+            jax.ShapeDtypeStruct((1, ffn_dim), f32),
+        ],
+        compiler_params=pltpu.CompilerParams(vmem_limit_bytes=60 * 2**20),
+        cost_estimate=pl.CostEstimate(flops=40_000_000_000, bytes_accessed=50_000_000, transcendentals=0),
+    )(mine, theirs, tokens, grad_hidden, grad_term, w_out, w_in, w_down, vec, bias_in, term_bias)
+
+
+def bit(place, which):
+    return (place // 2**which) % 2
+
+
+def flip(place, which):
+    return place + (1 - 2 * bit(place, which)) * 2**which
+
+
+def route(target, me, head):
+    low, high = bit(target, 0), bit(target, 1)
+    send = (1 - head) * ((low + bit(me, 0)) % 2) + head * ((high + bit(me, 1)) % 2)
+    return send, 2 * (target // 4) + (1 - head) * high + head * low
+
+
+def greet(partners):
+    barrier = pltpu.get_barrier_semaphore()
+    for partner in partners:
+        pl.semaphore_signal(barrier, inc=1, device_id=partner, device_id_type=pl.DeviceIdType.MESH)
+    pl.semaphore_wait(barrier, len(partners))
+
+
+def remote(source, target, send_sem, recv_sem, partner):
+    return pltpu.make_async_remote_copy(
+        src_ref=source,
+        dst_ref=target,
+        send_sem=send_sem,
+        recv_sem=recv_sem,
+        device_id=partner,
+        device_id_type=pl.DeviceIdType.MESH,
+    )
+
+
+def weights_kernel(
+    n_dp,
+    parts,
+    left_ref,
+    right_ref,
+    my_cols_ref,
+    their_cols_ref,
+    vec_ref,
+    keep_ref,
+    send_ref,
+    grads_ref,
+    vec_out_ref,
+    full_ref,
+    recv_ref,
+    both_ref,
+    vec_recv_ref,
+    send_sem,
+    recv_sem,
+    grad_send_sem,
+    grad_recv_sem,
+    vec_send_sem,
+    vec_recv_sem,
+    copy_sem,
+):
+    me, head = lax.axis_index("dp"), lax.axis_index("head")
+    other = (me, 1 - head)
+    step = pl.program_id(0)
+    steps = 2 * parts + 1
+    model_dim = left_ref.shape[2]
+    cols = model_dim // 2
+    half = my_cols_ref.shape[0]
+    down_rows = parts * model_dim // n_dp
+    rows = model_dim // n_dp
+    my_rows = grads_ref.at[pl.ds(pl.multiple_of(head * half, half), half)]
+    own_copy = pltpu.make_async_copy(my_cols_ref, my_rows, copy_sem.at[2])
+    grad_copy = remote(their_cols_ref, my_rows, grad_send_sem, grad_recv_sem, other)
+    vec_copy = remote(vec_ref, vec_recv_ref, vec_send_sem, vec_recv_sem, other)
+    my_half = pl.ds(pl.multiple_of(head * cols, LANES), cols)
+    other_half = pl.ds(pl.multiple_of((1 - head) * cols, LANES), cols)
+
+    def exchange(k):
+        return remote(full_ref.at[k % 2, :, other_half], recv_ref.at[k], send_sem.at[k], recv_sem.at[k], other)
+
+    @pl.when(step == 0)
+    def _():
+        greet([other])
+        grad_copy.start()
+        vec_copy.start()
+        own_copy.start()
+
+    @pl.when(step >= 2)
+    def _():
+        exchange(step - 2).wait_send()
+
+    full_ref[step % 2] = lax.dot_general(left_ref[0], right_ref[0], TN, preferred_element_type=f32).astype(bf16)
+    exchange(step).start()
+
+    def finish(k):
+        exchange(k).wait_recv()
+
+        def total(start, count):
+            return (
+                full_ref[k % 2, start : start + count, my_half].astype(f32)
+                + recv_ref[k, start : start + count, :].astype(f32)
+            ).astype(bf16)
+
+        @pl.when(k < parts)
+        def _():
+            count = model_dim // down_rows
+            for q in range(count):
+                send, place = route(k * count + q, me, head)
+                both_ref[send, place, :down_rows, :] = total(q * down_rows, down_rows)
+
+        @pl.when(k >= parts)
+        def _():
+            start = pl.multiple_of(down_rows + (k - parts) * rows, 16)
+            for d in range(n_dp):
+                send, place = route(d, me, head)
+                both_ref[send, place, pl.ds(start, rows), :] = total(d * rows, rows)
+
+    @pl.when(step >= 1)
+    def _():
+        finish(step - 1)
+
+    @pl.when(step == steps - 1)
+    def _():
+        finish(steps - 1)
+        copies = [
+            pltpu.make_async_copy(both_ref.at[0], keep_ref, copy_sem.at[0]),
+            pltpu.make_async_copy(both_ref.at[1], send_ref, copy_sem.at[1]),
+        ]
+        for copy in copies:
+            copy.start()
+        vec_copy.wait()
+        vec_out_ref[...] = vec_ref[...] + vec_recv_ref[...]
+        grad_copy.wait()
+        own_copy.wait()
+        exchange(steps - 2).wait_send()
+        exchange(steps - 1).wait_send()
+        for copy in copies:
+            copy.wait()
+
+
+def weights(n_dp, left, right, my_cols, their_cols, vec):
+    stack, half, model_dim = left.shape
+    parts = stack - 2
+    steps = 2 * parts + 1
+    cols = model_dim // 2
+    block_rows = (2 * parts + 1) * model_dim // n_dp
+    anywhere = pl.BlockSpec(memory_space=pl.ANY)
+
+    def left_map(j):
+        return (jnp.where(j < parts, j, jnp.where(j < 2 * parts, parts, parts + 1)), 0, 0)
+
+    def right_map(j):
+        return (jnp.where(j < parts, 0, j - parts + 1), 0, 0)
+
+    blocks = jax.ShapeDtypeStruct((n_dp // 2, block_rows, cols), bf16)
+    return pl.pallas_call(
+        partial(weights_kernel, n_dp, parts),
+        grid=(steps,),
+        in_specs=[
+            pl.BlockSpec((1, half, model_dim), left_map),
+            pl.BlockSpec((1, half, model_dim), right_map),
+            anywhere,
+            anywhere,
+            pl.BlockSpec(vec.shape, lambda j: (0, 0)),
+        ],
+        out_specs=[anywhere, anywhere, anywhere, pl.BlockSpec(vec.shape, lambda j: (0, 0))],
+        scratch_shapes=[
+            pltpu.VMEM((2, model_dim, model_dim), bf16),
+            pltpu.VMEM((steps, model_dim, cols), bf16),
+            pltpu.VMEM((2,) + blocks.shape, bf16),
+            pltpu.VMEM(vec.shape, f32),
+            pltpu.SemaphoreType.DMA((steps,)),
+            pltpu.SemaphoreType.DMA((steps,)),
+            pltpu.SemaphoreType.DMA,
+            pltpu.SemaphoreType.DMA,
+            pltpu.SemaphoreType.DMA,
+            pltpu.SemaphoreType.DMA,
+            pltpu.SemaphoreType.DMA((3,)),
+        ],
+        out_shape=[
+            blocks,
+            blocks,
+            jax.ShapeDtypeStruct((2 * half, my_cols.shape[1]), bf16),
+            jax.ShapeDtypeStruct(vec.shape, f32),
+        ],
+        compiler_params=pltpu.CompilerParams(
+            collective_id=0, has_side_effects=True, vmem_limit_bytes=48 * 2**20
+        ),
+        cost_estimate=pl.CostEstimate(flops=15_000_000_000, bytes_accessed=20_000_000, transcendentals=0),
+    )(left, right, my_cols, their_cols, vec)
+
+
+def halve_kernel(mine_ref, kept_ref, got_ref, keep_ref, send_ref):
+    mine = mine_ref[0]
+    total = (kept_ref[0].astype(f32) + got_ref[0].astype(f32)).astype(bf16)
+
+    @pl.when(mine == 0)
+    def _():
+        keep_ref[0] = total[0]
+        send_ref[0] = total[1]
+
+    @pl.when(mine == 1)
+    def _():
+        keep_ref[0] = total[1]
+        send_ref[0] = total[0]
+
+
+def halve(mine, kept, got):
+    count, rows, cols = kept.shape
+    pair = pl.BlockSpec((1, 2, rows, cols), lambda i, n: (i, 0, 0, 0))
+    one = pl.BlockSpec((1, rows, cols), lambda i, n: (i, 0, 0))
+    shape = jax.ShapeDtypeStruct((count // 2, rows, cols), bf16)
+    return pl.pallas_call(
+        halve_kernel,
+        grid_spec=pltpu.PrefetchScalarGridSpec(
+            num_scalar_prefetch=1, grid=(count // 2,), in_specs=[pair, pair], out_specs=[one, one]
+        ),
+        out_shape=[shape, shape],
+        cost_estimate=pl.CostEstimate(flops=1_000_000, bytes_accessed=6 * kept.size, transcendentals=0),
+    )(mine[None], kept.reshape(count // 2, 2, rows, cols), got.reshape(count // 2, 2, rows, cols))
+
+
+def projection_kernel(n_dp, rows_ref, raw_a_ref, raw_b_ref, keep_ref, send_ref, both_ref, sem):
+    me, head = lax.axis_index("dp"), lax.axis_index("head")
+    rows = both_ref.shape[2]
+    local_dim = both_ref.shape[3] // 3
+    begin = 0
+    for raw_ref in (raw_a_ref, raw_b_ref):
+        width = raw_ref.shape[1] // 3
+        for c in range(3):
+            grad = lax.dot_general(
+                rows_ref[...], raw_ref[:, c * width : (c + 1) * width], TN, preferred_element_type=f32
+            ).astype(bf16)
+            start = c * local_dim + begin
+            for d in range(n_dp):
+                send, place = route(d, me, head)
+                both_ref[send, place, :, start : start + width] = grad[d * rows : (d + 1) * rows]
+        begin += width
+    copies = [
+        pltpu.make_async_copy(both_ref.at[0], keep_ref, sem.at[0]),
+        pltpu.make_async_copy(both_ref.at[1], send_ref, sem.at[1]),
+    ]
+    for copy in copies:
+        copy.start()
+    for copy in copies:
+        copy.wait()
+
+
+def projection(n_dp, group_rows, raw_a, raw_b):
+    model_dim = group_rows.shape[1]
+    shape = (n_dp // 2, model_dim // n_dp, raw_a.shape[1] + raw_b.shape[1])
+    anywhere = pl.BlockSpec(memory_space=pl.ANY)
+    vmem = pl.BlockSpec(memory_space=pltpu.VMEM)
+    return pl.pallas_call(
+        partial(projection_kernel, n_dp),
+        in_specs=[vmem] * 3,
+        out_specs=[anywhere] * 2,
+        scratch_shapes=[pltpu.VMEM((2,) + shape, bf16), pltpu.SemaphoreType.DMA((2,))],
+        out_shape=[jax.ShapeDtypeStruct(shape, bf16)] * 2,
+        compiler_params=pltpu.CompilerParams(vmem_limit_bytes=48 * 2**20),
+        cost_estimate=pl.CostEstimate(flops=4_000_000_000, bytes_accessed=10_000_000, transcendentals=0),
+    )(group_rows, raw_a, raw_b)
+
+
+def last_kernel(
+    n_dp,
+    parts,
+    s_keep_ref,
+    s_got_ref,
+    q_keep_ref,
+    q_got_ref,
+    vec_ref,
+    down_ref,
+    in_ref,
+    out_ref,
+    qkv_ref,
+    vec_out_ref,
+    s_send_ref,
+    s_recv_ref,
+    s_hold_ref,
+    core_send_ref,
+    core_recv_ref,
+    q_send_refs,
+    q_recv_refs,
+    q_hold_refs,
+    vec_hold_ref,
+    vec_recv_ref,
+    vec_core_ref,
+    q_sems,
+    v_sems,
+    other_sems,
+):
+    bits = n_dp.bit_length() - 1
+    me, head = lax.axis_index("dp"), lax.axis_index("head")
+    other = (me, 1 - head)
+    along = [(flip(me, k), head) for k in range(bits)]
+    greet(along + [other])
+
+    top = bit(me, bits - 1)
+    for place in range(2):
+        total = s_keep_ref[place].astype(f32) + s_got_ref[place].astype(f32)
+
+        @pl.when(place == top)
+        def _():
+            s_hold_ref[...] = total
+
+        @pl.when(place != top)
+        def _():
+            s_send_ref[...] = total.astype(bf16)
+
+    s_copy = remote(s_send_ref, s_recv_ref, other_sems.at[0], other_sems.at[1], along[-1])
+    s_copy.start()
+
+    vec_hold_ref[0] = vec_ref[...]
+
+    def vec_copy(k):
+        return remote(vec_hold_ref.at[k], vec_recv_ref.at[k], v_sems.at[0, k], v_sems.at[1, k], along[k])
+
+    second = (flip(me, 1) * (1 - head) + flip(me, 0) * head, head)
+    second_bit = bit(me, 1) * (1 - head) + bit(me, 0) * head
+    stages = [(second_bit, second)] + [(bit(me, k), along[k]) for k in range(2, bits)]
+
+    def q_copy(s):
+        return remote(q_send_refs[s], q_recv_refs[s], q_sems.at[0, s], q_sems.at[1, s], stages[s][1])
+
+    def q_split(s, total_of):
+        mine = stages[s][0]
+        for p in range(q_send_refs[s].shape[0]):
+            q_send_refs[s][p] = total_of(2 * p + (1 - mine)).astype(bf16)
+        q_copy(s).start()
+        for p in range(q_send_refs[s].shape[0]):
+            q_hold_refs[s][p] = total_of(2 * p + mine)
+
+    q_split(0, lambda i: q_keep_ref[i].astype(f32) + q_got_ref[i].astype(f32))
+    vec_copy(0).start()
+
+    for k in range(bits):
+        vec_copy(k).wait()
+        total = vec_hold_ref[k] + vec_recv_ref[k]
+        if k < bits - 1:
+            vec_hold_ref[k + 1] = total
+            vec_copy(k + 1).start()
+        else:
+            vec_out_ref[...] = total
+        if k >= 1 and k < len(stages):
+            q_copy(k - 1).wait()
+            q_split(k, lambda i, k=k: q_hold_refs[k - 1][i] + q_recv_refs[k - 1][i].astype(f32))
+    core_vec = remote(vec_out_ref.at[pl.ds(8, 8)], vec_core_ref, other_sems.at[2], other_sems.at[3], other)
+    core_vec.start()
+
+    s_copy.wait()
+    rows = out_ref.shape[0]
+    down_rows = down_ref.shape[0]
+    cols = s_hold_ref.shape[1]
+
+    s_hold_ref[...] = s_hold_ref[...] + s_recv_ref[...].astype(f32)
+
+    def piece(start, count, who):
+        return s_hold_ref[pl.ds(pl.multiple_of(start + who * count, 8), count), :]
+
+    pieces = [(0, down_rows)] + [(2 * down_rows + 2 * rows * c, rows) for c in range(parts + 1)]
+    at = 0
+    for start, count in pieces:
+        core_send_ref[at : at + count, :] = piece(start, count, 1 - head)
+        at += count
+    core_copy = remote(core_send_ref, core_recv_ref, other_sems.at[4], other_sems.at[5], other)
+    core_copy.start()
+    my_half = pl.ds(pl.multiple_of(head * cols, LANES), cols)
+    other_half = pl.ds(pl.multiple_of((1 - head) * cols, LANES), cols)
+
+    def place_all(half, source):
+        down_ref[:, half] = source(0)
+        for c in range(parts):
+            shifted = pl.ds(pl.multiple_of(2 * cols * c + half.start, LANES), cols)
+            in_ref[:, shifted] = source(1 + c)
+        out_ref[:, half] = source(1 + parts)
+
+    place_all(my_half, lambda i: piece(*pieces[i], head))
+
+    last = len(stages) - 1
+    q_copy(last).wait()
+    qkv_ref[...] = q_hold_refs[last][0] + q_recv_refs[last][0].astype(f32)
+
+    core_vec.wait()
+    row = lax.broadcasted_iota(jnp.int32, vec_core_ref.shape, 0)
+    vec_out_ref[8:16] = vec_out_ref[8:16] + jnp.where(row >= 4, vec_core_ref[...], 0.0)
+    core_copy.wait()
+    starts = [0]
+    for _, count in pieces:
+        starts.append(starts[-1] + count)
+    place_all(other_half, lambda i: core_recv_ref[starts[i] : starts[i + 1], :])
+
+
+def last(n_dp, parts, s_keep, s_got, q_keep, q_got, vec):
+    bits = n_dp.bit_length() - 1
+    _, block_rows, cols = s_keep.shape
+    q_rows, q_cols = q_keep.shape[1:]
+    model_dim = vec.shape[1]
+    rows = model_dim // (2 * n_dp)
+    vmem = pl.BlockSpec(memory_space=pltpu.VMEM)
+    counts = [n_dp // 4 >> s for s in range(bits - 1)]
+
+    def stacks(kind):
+        return tuple(pltpu.VMEM((count, q_rows, q_cols), kind) for count in counts)
+
+    def shape(*dims):
+        return jax.ShapeDtypeStruct(dims, f32)
+
+    return pl.pallas_call(
+        partial(last_kernel, n_dp, parts),
+        in_specs=[vmem] * 5,
+        out_specs=[vmem] * 5,
+        scratch_shapes=[
+            pltpu.VMEM((block_rows, cols), bf16),
+            pltpu.VMEM((block_rows, cols), bf16),
+            pltpu.VMEM((block_rows, cols), f32),
+            pltpu.VMEM((block_rows // 2, cols), f32),
+            pltpu.VMEM((block_rows // 2, cols), f32),
+            stacks(bf16),
+            stacks(bf16),
+            stacks(f32),
+            pltpu.VMEM((bits,) + vec.shape, f32),
+            pltpu.VMEM((bits,) + vec.shape, f32),
+            pltpu.VMEM((8, model_dim), f32),
+            pltpu.SemaphoreType.DMA((2, bits - 1)),
+            pltpu.SemaphoreType.DMA((2, bits)),
+            pltpu.SemaphoreType.DMA((6,)),
+        ],
+        out_shape=[
+            shape(parts * rows, model_dim),
+            shape(rows, parts * model_dim),
+            shape(rows, model_dim),
+            shape(q_rows, q_cols),
+            shape(*vec.shape),
+        ],
+        compiler_params=pltpu.CompilerParams(
+            collective_id=1, has_side_effects=True, vmem_limit_bytes=32 * 2**20
+        ),
+        cost_estimate=pl.CostEstimate(flops=1_000_000_000, bytes_accessed=6_000_000, transcendentals=0),
+    )(s_keep, s_got, q_keep, q_got, vec)
 
 
 def take(array, index, axis=0):
@@ -337,90 +974,97 @@
     def their_half(rows):
         return lax.dynamic_slice_in_dim(rows, (1 - head) * half, half, 0)
 
-    token_mixed = both(my_half(attended), links.swap_head(their_half(attended)), 1)
-
-    inputs = tokens.astype(f32)
-    branch = jnp.dot(token_mixed, w_out, preferred_element_type=f32) + bias_out
-    normed_one, norm_one_back = jax.vjp(layer_norm, inputs + branch, ln1_gain, ln1_bias)
-    normed_low = normed_one.astype(bf16)
-    hidden_pre = jnp.dot(normed_low, w_in, preferred_element_type=f32) + bias_in
-    activated, gelu_back = jax.vjp(partial(jax.nn.gelu, approximate=False), hidden_pre)
-    active_low = activated.astype(bf16)
-    ffn_out = jnp.dot(active_low, w_down, preferred_element_type=f32) + bias_down
-    normed_two, norm_two_back = jax.vjp(layer_norm, normed_one + ffn_out, ln2_gain, ln2_bias)
-    term_logit = jnp.dot(normed_two, term_w, precision=highest) + term_bias[0]
-    term_weight = jax.nn.softplus(term_logit)
-    logit_grad = grad_term * jax.nn.sigmoid(term_logit)
-    two_grad = grad_hidden + logit_grad[:, None] * term_w[None, :]
-    term_w_local = jnp.dot(logit_grad, normed_two, precision=highest)
-    term_bias_local = jnp.sum(logit_grad)
-    resid_two_grad, gain_two_grad, shift_two_grad = norm_two_back(two_grad)
-    ffn_grad = resid_two_grad.astype(bf16)
-    down_local = lax.dot_general(active_low, ffn_grad, TN, preferred_element_type=f32).astype(bf16)
-    bias_down_local = jnp.sum(ffn_grad.astype(f32), axis=0)
-    active_grad = lax.dot_general(ffn_grad, w_down, NT, preferred_element_type=f32)
-    (pre_grad,) = gelu_back(active_grad)
-    pre_low = pre_grad.astype(bf16)
-    in_local = lax.dot_general(normed_low, pre_low, TN, preferred_element_type=f32).astype(bf16)
-    bias_in_local = jnp.sum(pre_low.astype(f32), axis=0)
-    one_grad = resid_two_grad + lax.dot_general(pre_low, w_in, NT, preferred_element_type=f32)
-    resid_one_grad, gain_one_grad, shift_one_grad = norm_one_back(one_grad)
-    branch_low = resid_one_grad.astype(bf16)
-    out_local = lax.dot_general(token_mixed, branch_low, TN, preferred_element_type=f32).astype(bf16)
-    bias_out_local = jnp.sum(branch_low.astype(f32), axis=0)
-    mixed_grad = lax.dot_general(branch_low, w_out, NT, preferred_element_type=f32).astype(bf16)
-
-    my_cols = lax.dynamic_slice_in_dim(mixed_grad, head * local_dim, local_dim, 1)
-    their_cols = lax.dynamic_slice_in_dim(mixed_grad, (1 - head) * local_dim, local_dim, 1)
-    head_grad = both(my_cols, links.swap_head(their_cols), 0)
-
-    raw_grad, raw_sums = attend_back(lengths, queries, key_rows, value_rows, head_grad, logs, seg_col, seg_row)
-
-    def blocks_of(partial_sum):
-        rows, cols = partial_sum.shape
-        return partial_sum.reshape(n_dp, 2, rows // (2 * n_dp), cols)
-
-    grad_down = links.scatter_dp(links.scatter_heads(blocks_of(down_local)))
-    grad_in = links.scatter_dp(links.scatter_heads(blocks_of(in_local)))
-    grad_out = links.scatter_dp(links.scatter_heads(blocks_of(out_local)))
-
-    input_grad = lax.dot_general(raw_grad, w_flat, NT, preferred_element_type=f32)
-    received = links.swap_head(their_half(input_grad).astype(bf16))
-    grad_tokens = resid_one_grad + my_half(input_grad) + received.astype(f32)
-    qkv_local = lax.dot_general(group_rows, raw_grad, TN, preferred_element_type=f32).astype(bf16)
-    grad_qkv = links.scatter_dp(qkv_local.reshape(n_dp, model_dim // n_dp, 3 * local_dim))
+    vec = jnp.stack([bias_out, ln1_gain, ln1_bias, bias_down, ln2_gain, ln2_bias, term_w, jnp.zeros_like(term_w)])
+    hidden_out, term_weight, left, right, resid_one_grad, my_cols, their_cols, sums, bias_in_local = middle(
+        my_half(attended),
+        links.swap_head(their_half(attended)),
+        tokens,
+        grad_hidden,
+        grad_term[:, None],
+        w_out,
+        w_in,
+        w_down,
+        vec,
+        bias_in[None, :],
+        term_bias[None, :],
+    )
+    parts = ffn_dim // model_dim
+    vec = jnp.concatenate([sums, bias_in_local.reshape(parts, model_dim)])
+    vec = jnp.pad(vec, ((0, 16 - vec.shape[0]), (0, 0)))
+    pairs = local_dim // LANES
+    split = pairs - 1
+    in_kernels = (model_dim // n_dp) % 16 == 0 and links.bits >= 3
+
+    def back(grads, own_lengths, first_pair, count):
+        return attend_back(
+            own_lengths, queries, key_rows, value_rows, grads, logs, seg_col, seg_row, first_pair, count
+        )
+
+    def tokens_grad(raw_a, raw_b):
+        w_a = w_qkv[:, :, : split * LANES].reshape(model_dim, -1)
+        w_b = w_qkv[:, :, split * LANES :].reshape(model_dim, -1)
+        grad = lax.dot_general(raw_a, w_a, NT, preferred_element_type=f32)
+        grad = grad + lax.dot_general(raw_b, w_b, NT, preferred_element_type=f32)
+        received = links.swap_head(their_half(grad).astype(bf16))
+        return resid_one_grad + my_half(grad) + received.astype(f32)
+
+    def value_sums(sums_a, sums_b):
+        rows = [
+            jnp.concatenate([x[:, c * x.shape[1] // 3 : (c + 1) * x.shape[1] // 3] for x in (sums_a, sums_b)], axis=1)
+            for c in (0, 2)
+        ]
+        return lax.dynamic_update_slice(
+            jnp.zeros((2, 2 * local_dim), f32), jnp.concatenate(rows), (jnp.int32(0), head * local_dim)
+        )
+
+    if in_kernels:
+        s_keep, s_send, head_grad, vec = weights(n_dp, left, right, my_cols, their_cols, vec)
+        s_got = links.permute(s_send, lambda d, h: (d ^ (1 if h == 0 else 2), h))
+        raw_a, sums_a = back(head_grad, lengths, 0, split)
+        s_keep, s_send = halve(jnp.where(head == 0, links.bit(1), links.bit(0)), s_keep, s_got)
+        s_got = links.permute(s_send, lambda d, h: (d ^ (2 if h == 0 else 1), h))
+        late_lengths, _ = lax.optimization_barrier((lengths, s_keep))
+        raw_b, sums_b = back(head_grad, late_lengths, split, 1)
+        for which in range(2, links.bits - 1):
+            s_keep, s_send = halve(links.bit(which), s_keep, s_got)
+            s_got = links.swap_bit(s_send, which)
+        q_keep, q_send = projection(n_dp, group_rows, raw_a, raw_b)
+        q_got = links.permute(q_send, lambda d, h: (d ^ (1 if h == 0 else 2), h))
+        grad_tokens = tokens_grad(raw_a, raw_b)
+        vec = lax.dynamic_update_slice(vec, value_sums(sums_a, sums_b), (12, 0))
+        grad_down, grad_in, grad_out, grad_qkv, vectors = last(n_dp, parts, s_keep, s_got, q_keep, q_got, vec)
+    else:
+        head_grad = both(my_cols, links.swap_head(their_cols), 0)
+        raw_a, sums_a = back(head_grad, lengths, 0, split)
+        raw_b, sums_b = back(head_grad, lengths, split, 1)
+
+        def product(i, j):
+            return lax.dot_general(left[i], right[j], TN, preferred_element_type=f32).astype(bf16)
+
+        def reduced(partial_sum):
+            rows, cols = partial_sum.shape
+            return links.scatter_dp(links.scatter_heads(partial_sum.reshape(n_dp, 2, rows // (2 * n_dp), cols)))
+
+        grad_down = reduced(jnp.concatenate([product(i, 0) for i in range(parts)]))
+        grad_in = reduced(jnp.concatenate([product(parts, 1 + i) for i in range(parts)], axis=1))
+        grad_out = reduced(product(parts + 1, parts + 1))
+        grad_tokens = tokens_grad(raw_a, raw_b)
+        raw = [x[:, c * x.shape[1] // 3 : (c + 1) * x.shape[1] // 3] for c in range(3) for x in (raw_a, raw_b)]
+        qkv_local = lax.dot_general(group_rows, jnp.concatenate(raw, axis=1), TN, preferred_element_type=f32)
+        grad_qkv = links.scatter_dp(qkv_local.astype(bf16).reshape(n_dp, model_dim // n_dp, 3 * local_dim))
+        vectors = links.total(lax.dynamic_update_slice(vec, value_sums(sums_a, sums_b), (12, 0)))
     grad_qkv = grad_qkv.reshape(model_dim // n_dp, 3, local_dim)
 
-    vectors = jnp.stack(
-        [
-            bias_out_local,
-            gain_one_grad,
-            shift_one_grad,
-            bias_down_local,
-            gain_two_grad,
-            shift_two_grad,
-            term_w_local,
-            jnp.full((model_dim,), term_bias_local),
-        ]
-    )
-    vectors = jnp.concatenate([vectors, bias_in_local.reshape(-1, model_dim)])
-    vectors = links.total(vectors)
     place = 2 * links.dp + head
     width = model_dim // (2 * n_dp)
-    mine = lax.dynamic_slice_in_dim(vectors[:8], place * width, width, 1)
+    mine = lax.dynamic_slice_in_dim(vectors, place * width, width, 1)
     in_width = ffn_dim // (2 * n_dp)
-    bias_in_mine = lax.dynamic_slice_in_dim(vectors[8:].reshape(-1), place * in_width, in_width, 0)
-
-    padded = lax.dynamic_update_slice(
-        jnp.zeros((2, 2 * local_dim), f32),
-        jnp.concatenate([raw_sums[:, :local_dim], raw_sums[:, 2 * local_dim :]]),
-        (jnp.int32(0), head * local_dim),
-    )
-    bias_qv_mine = lax.dynamic_slice_in_dim(links.total(padded), place * width, width, 1).T
+    bias_in_mine = lax.dynamic_slice_in_dim(vectors[8 : 8 + parts].reshape(-1), place * in_width, in_width, 0)
+    bias_qv_mine = mine[12:14].T
 
     return (
-        normed_two.astype(bf16),
-        term_weight,
+        hidden_out,
+        term_weight[:, 0],
         grad_tokens,
         grad_qkv,
         bias_qv_mine,

time: 373 us -> 294 us (0.79)
  Pallas kernels: 76.8 us -> 217 us
  matrix products: 124 us -> 17.3 us
  starting transfers between devices: 38.9 us -> 3.59 us
  waiting for transfers between devices: 41.6 us -> 12.3 us
  local copies, waits for them, and re-layouts: 46.2 us -> 21.5 us
  other arithmetic: 37.7 us -> 14.9 us
    pallas_call x1 -> x8, Pallas kernels: 45.7 us -> 184 us  [the longest x1 60.5 us: middle(): pl.pallas_call(middle_kernel, grid=(half // rows,), in_specs=[tile(local_...]
    dot_general x13 -> x2, matrix products: 116 us -> 13 us  [the longest x1 7.14 us: tokens_grad(): grad = lax.dot_general(raw_a, w_a, NT, preferred_element_type=f32)]
    ppermute x33 -> x7, starting transfers between devices: 38.9 us -> 3.59 us  [permute(): return lax.ppermute(array, AXES, pairs)]
    ppermute x33 -> x7, waiting for transfers between devices: 41.6 us -> 12.3 us  [permute(): return lax.ppermute(array, AXES, pairs)]
    reduce_sum x8 -> x0, other arithmetic: 10.5 us -> none  [the longest x2 5.34 us: layer_norm(): center = resid - jnp.mean(resid, axis=-1, keepdims=True)]
    convert_element_type x7 -> x0, other arithmetic: 10.1 us -> none  [the longest x3 6.58 us: scatter_heads(): (take(blocks, self.head, 1).astype(f32) + got.astype(f32)).astype(bf16)]
    unnamed x118 -> x60, local copies, waits for them, and re-layouts: 19.9 us -> 9.95 us
    squeeze x7 -> x0, local copies, waits for them, and re-layouts: 7.58 us -> none  [take(): return lax.dynamic_index_in_dim(array, index, axis, keepdims=False)]
  transfers between devices with their start and end apart: 33 -> 7, of which waited for: 13 -> 3; matrix products, arithmetic and copies ran while one was open for 21% -> 10% of each run, Pallas kernels for 12% -> 16%
where the time goes in v2:
time: 294 us; the launch traced here: 289 us
  Pallas kernels  217 us (74%)
  local copies, waits for them, and re-layouts  21.5 us (7%)
  matrix products  17.3 us (6%)
  other arithmetic  14.9 us (5%)
  waiting for transfers between devices  12.3 us (4%)
  starting transfers between devices  3.59 us (1%)
    pallas_call x1, Pallas kernels, middle(): pl.pallas_call(middle_kernel, grid=(half // rows,), in_specs=[tile(local_...  60.5 us
    pallas_call x2, Pallas kernels, attend_back(): pl.pallas_call(partial(attend_back_kernel, first_pair), grid_spec=pltpu.P...  55.4 us
    pallas_call x1, Pallas kernels, attend(): pl.pallas_call(attend_kernel, grid_spec=pltpu.PrefetchScalarGridSpec(num_...  33.7 us
    pallas_call x1, Pallas kernels, last(): pl.pallas_call(partial(last_kernel, n_dp, parts), in_specs=[vmem] * 5, ou...  30.2 us
    pallas_call x1, Pallas kernels, weights(): pl.pallas_call(partial(weights_kernel, n_dp, parts), grid=(steps,), in_sp...  21.3 us
    ppermute x7, waiting for transfers between devices, permute(): return lax.ppermute(array, AXES, pairs)  12.3 us
    unnamed x60, local copies, waits for them, and re-layouts  9.95 us
    pallas_call x1, Pallas kernels, projection(): pl.pallas_call(partial(projection_kernel, n_dp), in_specs=[vmem] * 3, out...  8.36 us
  transfers between devices with their start and end apart: 7, of which 3 were waited for; matrix products, arithmetic and copies ran while one was open for 10% of the time, Pallas kernels for 16%

profile of v2, /device:TPU:0, one launch (start us, length us, event | category | flops | bytes accessed | tf_op | source)
XLA Modules:
  0.0 289.1 jit_solution(6760396092244678214)
XLA Ops:
  0.7 0.5 collective-permute-start
  1.2 2.6 copy.43
  4.0 0.1 reduce.2
  4.2 0.3 collective-permute-done
  4.6 3.3 %maximum_select_fusion.rows_ref = bf16[2048,768]{1,0:T(8,128)(2,1)S(1)} fusion(bf16[1024,768]{1,0:T(8,128)(2,1)} %collective-permute-done, bf16[1024,768]{1,0:T(8,128)(2,1)} %tokens_ref.1, pred[]{:T(512)S(6)} %eq.4), kind=kLoop, calls=%fused_computation.7 | loop fusion | flops 14155776 | bytes 6291457 | tf_op jit(solution)/shard_map/jit(_where)/select_n | solution.py:957
  7.9 4.3 %fusion.6 = f32[2048,1152]{1,0:T(8,128)S(1)} fusion(bf16[2048,768]{1,0:T(8,128)(2,1)S(1)} %maximum_select_fusion.rows_ref, bf16[768,1152]{0,1:T(8,128)(2,1)S(1)} %bitcast.46), kind=kOutput, calls=%fused_computation.32 | convolution fusion | flops 3623878656 | bytes 14352384 | tf_op jit(solution)/shard_map/dot_general | solution.py:965
  12.2 0.2 slice.101.k_ref
  12.4 1.8 fusion
  14.3 0.3 broadcast_in_dim.32.segc_ref
  14.6 33.7 %shard_map.305 = (bf16[2048,384]{1,0:T(8,128)(2,1)S(1)}, f32[8,2048]{1,0:T(8,128)S(1)}) custom-call(s32[1,32]{1,0:T(1,128)S(1)} %copy-done.6, bf16[2048,384]{1,0:T(8,128)(2,1)S(1)} %get-tuple-element.133.q_ref, bf16[2048,384]{1,0:T(8,128)(2,1)S(1)} %slice.101.k_ref, bf16[2048,384]{1,0:T(8,128)(2,1)} %get-tuple-element.132.v_ref, ...), custom_call_target="tpu_custom_call" | custom-call | flops 20000000000 | bytes 8000000 | tf_op jit(solution)/shard_map/pallas_call | solution.py:94
  48.5 1.0 constant_dynamic-slice_fusion.1
  49.6 0.4 collective-permute-start.1
  50.0 0.2 copy-done.13
  50.3 1.1 slice.89
  51.4 1.1 copy.45.term_ref
  53.3 0.7 stack.31.vec_ref
  53.9 60.5 %shard_map.306 = (bf16[1024,768]{1,0:T(8,128)(2,1)}, f32[1024,1]{1,0:T(8,128)}, bf16[6,1024,768]{2,1,0:T(8,128)(2,1)}, bf16[6,1024,768]{2,1,0:T(8,128)(2,1)}, f3...) custom-call(bf16[1024,384]{1,0:T(8,128)(2,1)} %get-tuple-element.135, ...), custom_call_target="tpu_custom_call" | custom-call | flops 40000000000 | bytes 50000000 | tf_op jit(solution)/shard_map/pallas_call | solution.py:378
  114.5 0.5 broadcast.17
  115.0 1.4 reduce.9
  116.4 0.7 select_maximum_fusion.vec_ref
  117.1 1.1 copy-done.9
  118.3 1.1 copy-done.10
  119.4 21.3 %shard_map.307 = (bf16[8,432,384]{2,1,0:T(8,128)(2,1)S(1)}, bf16[8,432,384]{2,1,0:T(8,128)(2,1)}, bf16[2048,384]{1,0:T(8,128)(2,1)S(1)}, f32[16,768]{1,0:T(8,128)S(1)}) custom-call(bf16[6,1024,768]{2,1,0:T(8,128)(2,1)} %get-tuple-element.52.left_ref, bf16[6,1024,768]{2,1,0:T(8,128)(2,1)} %get-tuple-element.53.right_ref, bf16[1024,384]{1,0:T(8,128)(2,1)S(1)} %copy-done.9, ...), custom_call_target="tpu_custom_call" | custom-call | flops 15000000512 | bytes 20000000 | tf_op jit(solution)/shard_map/pallas_call | solution.py:572
  140.7 1.5 copy-done.1
  142.2 1.2 copy-done.8
  143.4 0.9 collective-permute-start.2
  144.3 35.3 %shard_map.308 = (bf16[2048,768]{1,0:T(8,128)(2,1)}, f32[1,768]{1,0:T(1,128)}) custom-call(s32[1,32]{1,0:T(1,128)} %lengths_ref.4, bf16[2048,384]{1,0:T(8,128)(2,1)} %copy-done.3, bf16[2048,384]{1,0:T(8,128)(2,1)} %copy-done.2, bf16[2048,384]{1,0:T(8,128)(2,1)} %get-tuple-element.132.v_ref, bf16[2048,384]{1,0:T(8,128)(2,1)} %copy-done.8, ...), custom_call_target="tpu_custom_call" | custom-call | flops 28000000000 | bytes 8000000 | tf_op jit(solution)/shard_map/pallas_call | solution.py:184
  179.6 7.1 %fusion.7 = f32[2048,768]{1,0:T(8,128)} fusion(bf16[2048,768]{1,0:T(8,128)(2,1)} %get-tuple-element.60.raw_a_ref, bf16[768,768]{0,1:T(8,128)(2,1)S(1)} %bitcast.49), kind=kOutput, calls=%fused_computation.33 | convolution fusion | flops 2415919104 | bytes 10616832 | tf_op jit(solution)/shard_map/dot_general | solution.py:1006
  186.7 5.0 %shard_map.309 = (bf16[4,432,384]{2,1,0:T(8,128)(2,1)}, bf16[4,432,384]{2,1,0:T(8,128)(2,1)}) custom-call(s32[1]{0:T(128)} %bitcast.6.mine_ref, bf16[4,2,432,384]{3,2,1,0:T(8,128)(2,1)} %bitcast.41, bf16[4,2,432,384]{3,2,1,0:T(8,128)(2,1)} %bitcast.8.got_ref), custom_call_target="tpu_custom_call" | custom-call | flops 1000000 | bytes 7962624 | tf_op jit(solution)/shard_map/pallas_call | solution.py:629
  191.8 20.1 %shard_map.310 = (bf16[2048,384]{1,0:T(8,128)(2,1)}, f32[1,384]{1,0:T(1,128)}) custom-call(s32[1,32]{1,0:T(1,128)} %lengths_ref.4, bf16[2048,384]{1,0:T(8,128)(2,1)} %copy-done.3, bf16[2048,384]{1,0:T(8,128)(2,1)} %copy-done.2, bf16[2048,384]{1,0:T(8,128)(2,1)} %get-tuple-element.132.v_ref, bf16[2048,384]{1,0:T(8,128)(2,1)} %copy-done.8, ...), custom_call_target="tpu_custom_call" | custom-call | flops 14000000000 | bytes 4000000 | tf_op jit(solution)/shard_map/pallas_call | solution.py:184
  212.0 5.8 %convolution_add_fusion = f32[2048,768]{1,0:T(8,128)} fusion(f32[2048,768]{1,0:T(8,128)S(1)} %bitcast.45, bf16[2048,384]{1,0:T(8,128)(2,1)} %get-tuple-element.65.raw_b_ref, bf16[768,384]{0,1:T(8,128)(2,1)S(1)} %bitcast.47), kind=kOutput, calls=%fused_computation | convolution fusion | flops 1209532416 | bytes 14745600 | tf_op jit(solution)/shard_map/dot_general | solution.py:1007
  217.9 3.3 %dynamic-slice_convert_fusion = bf16[1024,768]{1,0:T(8,128)(2,1)} fusion(f32[2048,768]{1,0:T(8,128)} %convolution_add_fusion, s32[]{:T(128)S(6)} %select_n.32), kind=kLoop, calls=%fused_computation.9 | loop fusion | bytes 3145732 | tf_op jit(solution)/shard_map/convert_element_type | solution.py:1008
  221.2 8.4 %shard_map.312 = (bf16[8,48,1152]{2,1,0:T(8,128)(2,1)S(1)}, bf16[8,48,1152]{2,1,0:T(8,128)(2,1)S(1)}) custom-call(bf16[2048,768]{1,0:T(8,128)(2,1)} %copy-done.14, bf16[2048,768]{1,0:T(8,128)(2,1)} %get-tuple-element.60.raw_a_ref, bf16[2048,384]{1,0:T(8,128)(2,1)S(1)} %copy-done), custom_call_target="tpu_custom_call" | custom-call | flops 4000000000 | bytes 10000000 | tf_op jit(solution)/shard_map/pallas_call | solution.py:670
  229.6 1.7 collective-permute-start.6
  231.3 1.8 reduce.3
  233.1 2.9 shard_map.311
  236.1 5.5 %convert_add_fusion = f32[1024,768]{1,0:T(8,128)} fusion(bf16[1024,768]{1,0:T(8,128)(2,1)} %collective-permute-done.3, f32[1024,768]{1,0:T(8,128)} %get-tuple-element.51, f32[2048,768]{1,0:T(8,128)} %convolution_add_fusion, s32[]{:T(128)S(6)} %select_n.31), kind=kLoop, calls=%fused_computation.8 | loop fusion | flops 2359296 | bytes 11010052 | tf_op jit(solution)/shard_map/add | solution.py:1009
  241.6 1.1 collective-permute-done.6.q_got_ref
  242.7 10.9 %collective-permute-done.5.s_got_ref = bf16[2,432,384]{2,1,0:T(8,128)(2,1)S(1)} collective-permute-done((bf16[2,432,384]{2,1,0:T(8,128)(2,1)}, bf16[2,432,384]{2,1,0:T(8,128)(2,1)S(1)}, u32[]{:S(2)}, u32[]{:S(2)}) %collective-permute-start.5) | collective-permute-done | bytes 663584 | tf_op jit(solution)/shard_map/ppermute | solution.py:879
  253.6 30.2 %shard_map.313 = (f32[96,768]{1,0:T(8,128)S(1)}, f32[24,3072]{1,0:T(8,128)S(1)}, f32[24,768]{1,0:T(8,128)S(1)}, f32[48,1152]{1,0:T(8,128)S(1)}, f32[16,768]{1,0:T(8,128)S(1)}) custom-call(bf16[2,432,384]{2,1,0:T(8,128)(2,1)S(1)} %copy-done.7, bf16[2,432,384]{2,1,0:T(8,128)(2,1)S(1)} %collective-permute-done.5.s_got_ref, ...), custom_call_target="tpu_custom_call" | custom-call | flops 1000000000 | bytes 6000000 | tf_op jit(solution)/shard_map/pallas_call | solution.py:825
  283.8 0.5 slice.84
  284.3 0.7 copy.51
  285.0 0.6 dynamic-slice_bitcast_fusion
  285.7 0.6 dynamic_slice.23
  286.2 0.6 dynamic-slice_bitcast_fusion.1
  286.9 0.6 copy.58
  287.5 0.7 copy.59
  288.2 0.7 copy.60
  (81 shorter events, 0.7 us)
Async XLA Ops:
  0.7 3.2 %copy-start.6 = (s32[1,32]{1,0:T(1,128)S(1)}, s32[1,32]{1,0:T(1,128)}, u32[]{:S(2)}) copy-start(s32[1,32]{1,0:T(1,128)} %lengths_ref.4) | copy-start | bytes 388
  0.7 3.4 %copy-start.23 = (f32[384,2]{0,1:T(2,128)S(1)}, f32[384,2]{0,1:T(2,128)}, u32[]{:S(2)}) copy-start(f32[384,2]{0,1:T(2,128)} %param.21) | copy-start | bytes 9220
  0.7 3.9 %collective-permute-start = (bf16[1024,768]{1,0:T(8,128)(2,1)}, bf16[1024,768]{1,0:T(8,128)(2,1)}, u32[]{:S(2)}, u32[]{:S(2)}) collective-permute-start(bf16[1024,768]{1,0:T(8,128)(2,1)} %tokens_ref.1), channel_id=1, source_target_pairs={{0,1},{1,0},{2,3},{3,2},{4,5},{5,4},{6,7},{7,6},{8,9},{9,8},{10,11... | collective-permute-start | bytes 4718600 | tf_op jit(solution)/shard_map/ppermute | solution.py:879
  3.8 4.0 %copy-start.12 = (bf16[768,3,384]{0,2,1:T(8,128)(2,1)}, bf16[768,3,384]{0,2,1:T(8,128)(2,1)S(1)}, u32[]{:S(2)}) copy-start(bf16[768,3,384]{0,2,1:T(8,128)(2,1)S(1)} %copy.43) | copy-start | bytes 5308420
  7.9 4.4 %copy-start.14 = (bf16[2048,768]{1,0:T(8,128)(2,1)}, bf16[2048,768]{1,0:T(8,128)(2,1)S(1)}, u32[]{:S(2)}) copy-start(bf16[2048,768]{1,0:T(8,128)(2,1)S(1)} %maximum_select_fusion.rows_ref) | copy-start | bytes 9437188
  12.4 2.2 copy-start.2
  14.3 34.1 %copy-start.3 = (bf16[2048,384]{1,0:T(8,128)(2,1)}, bf16[2048,384]{1,0:T(8,128)(2,1)S(1)}, u32[]{:S(2)}) copy-start(bf16[2048,384]{1,0:T(8,128)(2,1)S(1)} %get-tuple-element.133.q_ref) | copy-start | bytes 4718596
  14.6 33.8 %copy-start.4 = (s32[2048,128]{1,0:T(8,128)}, s32[2048,128]{1,0:T(8,128)S(1)}, u32[]{:S(2)}) copy-start(s32[2048,128]{1,0:T(8,128)S(1)} %broadcast_in_dim.32.segc_ref) | copy-start | bytes 3145732
  14.6 33.8 %copy-start.5 = (s32[8,2048]{1,0:T(8,128)}, s32[8,2048]{1,0:T(8,128)S(1)}, u32[]{:S(2)}) copy-start(s32[8,2048]{1,0:T(8,128)S(1)} %broadcast_in_dim.33.segr_ref) | copy-start | bytes 196612
  48.4 1.2 copy-start.11
  48.4 1.8 copy-start.13
  48.4 3.0 %copy-start.15 = (f32[1024]{0:T(1024)S(1)}, f32[1024]{0:T(1024)}, u32[]{:S(2)}) copy-start(f32[1024]{0:T(1024)} %param.35) | copy-start | bytes 12292
  48.4 4.0 %copy-start.16 = (f32[768]{0:T(1024)S(1)}, f32[768]{0:T(1024)}, u32[]{:S(2)}) copy-start(f32[768]{0:T(1024)} %param.23) | copy-start | bytes 9220
  48.5 4.0 %copy-start.17 = (f32[768]{0:T(1024)S(1)}, f32[768]{0:T(1024)}, u32[]{:S(2)}) copy-start(f32[768]{0:T(1024)} %param.24) | copy-start | bytes 9220
  48.5 4.0 %copy-start.18 = (f32[768]{0:T(1024)S(1)}, f32[768]{0:T(1024)}, u32[]{:S(2)}) copy-start(f32[768]{0:T(1024)} %param.25) | copy-start | bytes 9220
  48.5 4.0 %copy-start.19 = (f32[768]{0:T(1024)S(1)}, f32[768]{0:T(1024)}, u32[]{:S(2)}) copy-start(f32[768]{0:T(1024)} %param.29) | copy-start | bytes 9220
  48.5 4.1 %copy-start.20 = (f32[768]{0:T(1024)S(1)}, f32[768]{0:T(1024)}, u32[]{:S(2)}) copy-start(f32[768]{0:T(1024)} %param.30) | copy-start | bytes 9220
  48.5 4.1 %copy-start.21 = (f32[768]{0:T(1024)S(1)}, f32[768]{0:T(1024)}, u32[]{:S(2)}) copy-start(f32[768]{0:T(1024)} %param.31) | copy-start | bytes 9220
  48.5 4.1 %copy-start.22 = (f32[768]{0:T(1024)S(1)}, f32[768]{0:T(1024)}, u32[]{:S(2)}) copy-start(f32[768]{0:T(1024)} %param.32) | copy-start | bytes 9220
  49.6 4.4 %collective-permute-start.1 = (bf16[1024,384]{1,0:T(8,128)(2,1)S(1)}, bf16[1024,384]{1,0:T(8,128)(2,1)}, u32[]{:S(2)}, u32[]{:S(2)}) collective-permute-start(bf16[1024,384]{1,0:T(8,128)(2,1)S(1)} %get-tuple-element.134), channel_id=1, source_target_pairs={{0,1},{1,0},{2,3},{3,2},{4,5},{5,4},{6,7},{7,6},{8,9},{9,8},{10,11... | collective-permute-start | bytes 2359304 | tf_op jit(solution)/shard_map/ppermute | solution.py:879
  117.1 1.1 copy-start.9
  118.3 1.1 copy-start.10
  140.7 1.5 copy-start.1
  142.2 1.2 copy-start.8
  143.4 43.4 %collective-permute-start.2 = (bf16[8,432,384]{2,1,0:T(8,128)(2,1)}, bf16[8,432,384]{2,1,0:T(8,128)(2,1)}, u32[]{:S(2)}, u32[]{:S(2)}) collective-permute-start(bf16[8,432,384]{2,1,0:T(8,128)(2,1)} %get-tuple-element.62), channel_id=1, source_target_pairs={{0,2},{1,5},{2,0},{3,7},{4,6},{5,1},{6,4},{7,3},{8,10},{9,13},{10,... | collective-permute-start | bytes 7962632 | tf_op jit(solution)/shard_map/ppermute | solution.py:879
  191.8 20.2 %slice-start = ((s8[6291456]{0:T(1024)(128)(4,1)}), s8[4194304]{0:T(1024)(128)(4,1)S(1)}, s32[]{:S(2)}) async-start(s8[6291456]{0:T(1024)(128)(4,1)} %bitcast.44), calls=%async_computation | async-start | bytes 8388608
  191.8 20.2 %slice-start.1 = ((s8[6291456]{0:T(1024)(128)(4,1)}), s8[2097152]{0:T(1024)(128)(4,1)S(1)}, s32[]{:S(2)}) async-start(s8[6291456]{0:T(1024)(128)(4,1)} %bitcast.44), calls=%async_computation.1 | async-start | bytes 4194304
  211.9 21.2 %collective-permute-start.4 = (bf16[4,432,384]{2,1,0:T(8,128)(2,1)}, bf16[4,432,384]{2,1,0:T(8,128)(2,1)}, u32[]{:S(2)}, u32[]{:S(2)}) collective-permute-start(bf16[4,432,384]{2,1,0:T(8,128)(2,1)} %get-tuple-element.66), channel_id=1, source_target_pairs={{0,4},{1,3},{2,6},{3,1},{4,0},{5,7},{6,2},{7,5},{8,12},{9,11},{10,... | collective-permute-start | bytes 3981320 | tf_op jit(solution)/shard_map/ppermute | solution.py:879
  217.9 3.4 %copy-start = (bf16[2048,384]{1,0:T(8,128)(2,1)S(1)}, bf16[2048,384]{1,0:T(8,128)(2,1)}, u32[]{:S(2)}) copy-start(bf16[2048,384]{1,0:T(8,128)(2,1)} %get-tuple-element.65.raw_b_ref) | copy-start | bytes 4718596
  221.2 14.9 %collective-permute-start.3 = (bf16[1024,768]{1,0:T(8,128)(2,1)}, bf16[1024,768]{1,0:T(8,128)(2,1)}, u32[]{:S(2)}, u32[]{:S(2)}) collective-permute-start(bf16[1024,768]{1,0:T(8,128)(2,1)} %dynamic-slice_convert_fusion), channel_id=1, source_target_pairs={{0,1},{1,0},{2,3},{3,2},{4,5},{5,4},{6,7},{7,6},{8,9},{9,8},{10,11... | collective-permute-start | bytes 4718600 | tf_op jit(solution)/shard_map/ppermute | solution.py:879
  221.2 10.1 %copy-start.24 = (f32[1,768]{1,0:T(1,128)S(1)}, f32[1,768]{1,0:T(1,128)}, u32[]{:S(2)}) copy-start(f32[1,768]{1,0:T(1,128)} %get-tuple-element.72) | copy-start | bytes 9220
  229.6 6.4 %copy-start.25 = (f32[1,384]{1,0:T(1,128)S(1)}, f32[1,384]{1,0:T(1,128)}, u32[]{:S(2)}) copy-start(f32[1,384]{1,0:T(1,128)} %get-tuple-element.73) | copy-start | bytes 4612
  229.6 13.1 %collective-permute-start.6 = (bf16[8,48,1152]{2,1,0:T(8,128)(2,1)S(1)}, bf16[8,48,1152]{2,1,0:T(8,128)(2,1)S(1)}, u32[]{:S(2)}, u32[]{:S(2)}) collective-permute-start(bf16[8,48,1152]{2,1,0:T(8,128)(2,1)S(1)} %get-tuple-element.70), channel_id=1, source_target_pairs={{0,2},{1,5},{2,0},{3,7},{4,6},{5,1},{6,4},{7,3},{8,10},{9,13},{10,... | collective-permute-start | bytes 2654216 | tf_op jit(solution)/shard_map/ppermute | solution.py:879
  236.0 17.6 %collective-permute-start.5 = (bf16[2,432,384]{2,1,0:T(8,128)(2,1)}, bf16[2,432,384]{2,1,0:T(8,128)(2,1)S(1)}, u32[]{:S(2)}, u32[]{:S(2)}) collective-permute-start(bf16[2,432,384]{2,1,0:T(8,128)(2,1)} %get-tuple-element.68), channel_id=1, source_target_pairs={{0,8},{1,9},{2,10},{3,11},{4,12},{5,13},{6,14},{7,15},{8,0},{9,1},... | collective-permute-start | bytes 1990664 | tf_op jit(solution)/shard_map/ppermute | solution.py:879
  236.1 17.6 %copy-start.7 = (bf16[2,432,384]{2,1,0:T(8,128)(2,1)S(1)}, bf16[2,432,384]{2,1,0:T(8,128)(2,1)}, u32[]{:S(2)}) copy-start(bf16[2,432,384]{2,1,0:T(8,128)(2,1)} %get-tuple-element.67.s_keep_ref) | copy-start | bytes 1990660
